TPU v7x, 32 devices: a whole 2x2x4 slice. The times are simulated.
32 devices in a mesh: dp: 4 (over z), wide: 8 (over y, x, core).
Axes of the slice: x: 2, y: 2, z: 4, core: 2. Of those that a mesh axis runs over, the one named last changes fastest.
Arguments:
- tokens: bfloat16 [32768, 1024], P(('dp', 'wide')), may hold values from -6 to 6
- cotangent: bfloat16 [32768, 1024], P(('dp', 'wide')), may hold values from -6 to 6
- lengths: int32 [32, 2], P(('dp', 'wide')), may hold values from 0 to 1024, as said below
- in_weight: bfloat16 [1024, 3072], P(('dp', 'wide')), may hold values from -0.1875 to 0.1875
- query_bias: bfloat16 [1024], P(('dp', 'wide')), may hold values from -3 to 3
- value_bias: bfloat16 [1024], P(('dp', 'wide')), may hold values from -3 to 3
- out_weight: bfloat16 [1024, 1024], P(('dp', 'wide')), may hold values from -0.1875 to 0.1875
- out_bias: bfloat16 [1024], P(('dp', 'wide')), may hold values from -3 to 3
- head_scale: bfloat16 [16], replicated, may hold values from 0.29882812 to 3
- pre_gain: bfloat16 [1024], P(('dp', 'wide')), may hold values from 0.25 to 1.75
- pre_bias: bfloat16 [1024], P(('dp', 'wide')), may hold values from -3 to 3
- post_gain: bfloat16 [1024], P(('dp', 'wide')), may hold values from 0.25 to 1.75
- post_bias: bfloat16 [1024], P(('dp', 'wide')), may hold values from -3 to 3
- feed_gain: bfloat16 [1024], P(('dp', 'wide')), may hold values from 0.25 to 1.75
- feed_bias: bfloat16 [1024], P(('dp', 'wide')), may hold values from -3 to 3
- up_weight: bfloat16 [1024, 4096], P(None, 'wide'), may hold values from -0.1875 to 0.1875
- up_bias: bfloat16 [4096], P('wide'), may hold values from -3 to 3
- mid_gain: bfloat16 [4096], P('wide'), may hold values from 0.25 to 1.75
- mid_bias: bfloat16 [4096], P('wide'), may hold values from -3 to 3
- down_weight: bfloat16 [4096, 1024], P('wide'), may hold values from -0.09375 to 0.09375
- down_bias: bfloat16 [1024], replicated, may hold values from -3 to 3
Outputs:
- mixed: bfloat16 [32768, 1024], P(('dp', 'wide'))
- tokens_grad: bfloat16 [32768, 1024], P(('dp', 'wide'))
- in_weight_grad: float32 [1024, 3072], P(('dp', 'wide'))
- query_bias_grad: float32 [1024], P(('dp', 'wide'))
- value_bias_grad: float32 [1024], P(('dp', 'wide'))
- out_weight_grad: float32 [1024, 1024], P(('dp', 'wide'))
- out_bias_grad: float32 [1024], P(('dp', 'wide'))
- head_scale_grad: float32 [16], replicated
- pre_gain_grad: float32 [1024], P(('dp', 'wide'))
- pre_bias_grad: float32 [1024], P(('dp', 'wide'))
- post_gain_grad: float32 [1024], P(('dp', 'wide'))
- post_bias_grad: float32 [1024], P(('dp', 'wide'))
- feed_gain_grad: float32 [1024], P(('dp', 'wide'))
- feed_bias_grad: float32 [1024], P(('dp', 'wide'))
- up_weight_grad: float32 [1024, 4096], P(None, 'wide')
- up_bias_grad: float32 [4096], P('wide')
- mid_gain_grad: float32 [4096], P('wide')
- mid_bias_grad: float32 [4096], P('wide')
- down_weight_grad: float32 [4096, 1024], P('wide')
- down_bias_grad: float32 [1024], replicated
Inputs may be any that keep to these rules, and one draw needn't show every extreme that they name: `lengths`: each pack holds either one sequence of 1024 rows and a 0, or two sequences of 512 rows; both kinds occur in every draw.
All inputs are finite; a program needn't handle non-finite values.
Results may differ from a plain program's by a relative error of at most 0.017.
Values may be sent and summed in bfloat16 or wider, within the bound.
A program may use at most 320 MiB of HBM per device.

v0:
```python
import functools

import jax
import jax.numpy as jnp
from jax import lax
from jax.experimental import pallas as pl
from jax.experimental.pallas import tpu as pltpu
from jax.sharding import PartitionSpec as P

EPS = 1e-05
ROOT_HALF = 0.7071067811865476
INV_ROOT_TAU = 0.3989422804014327
LOG2E = 1.4426950408889634
MASKED = -1e30
BF = jnp.bfloat16
F32 = jnp.float32
TILE = 256
UNITS = 512
SLIM = 64
MESH = pl.DeviceIdType.MESH
VMEM_LIMIT = 62 * 1024 * 1024
ANY = pl.BlockSpec(memory_space=pl.ANY)


def dot_nn(left, right):
    return lax.dot_general(left, right, (((1,), (0,)), ((), ())), preferred_element_type=F32)


def dot_nt(left, right):
    return lax.dot_general(left, right, (((1,), (1,)), ((), ())), preferred_element_type=F32)


def dot_tn(left, right):
    return lax.dot_general(left, right, (((0,), (0,)), ((), ())), preferred_element_type=F32)


def params(**more):
    return pltpu.CompilerParams(
        dimension_semantics=("arbitrary",), vmem_limit_bytes=VMEM_LIMIT, **more
    )


def whole(shape):
    zeros = (0,) * len(shape)
    return pl.BlockSpec(shape, lambda *_: zeros, pipeline_mode=pl.Buffered(1))


def row_norm(values):
    center = values - jnp.mean(values, axis=-1, keepdims=True)
    inv = lax.rsqrt(jnp.mean(center * center, axis=-1, keepdims=True) + EPS)
    return center * inv, inv


def norm_back(grad, gain, normed, inv):
    scaled = grad * gain
    first = jnp.mean(scaled, axis=-1, keepdims=True)
    cross = jnp.mean(scaled * normed, axis=-1, keepdims=True)
    return inv * (scaled - first - normed * cross)


def column_sum(values):
    return jnp.sum(values, axis=0, keepdims=True)


def lane_fold(values):
    total = values[:, :128]
    for start in range(128, values.shape[1], 128):
        total = total + values[:, start : start + 128]
    return total


def cross_flag(lengths_ref, rows_ref):
    return jnp.where(lengths_ref[0, 0] == rows_ref.shape[0], 0.0, MASKED)


def stacked(value, low_lanes):
    zero = jnp.zeros_like(value)
    return jnp.concatenate(
        [jnp.where(low_lanes, value, zero), jnp.where(low_lanes, zero, value)], axis=0
    )


def attention_pair(cross, q_ref, k_ref, v_ref, scale, scaled_ref, out_ref, lse_ref, vext_ref):
    rows = q_ref.shape[0]
    half = rows // 2
    factor = LOG2E * 64 ** (-0.5)
    low_lanes = lax.broadcasted_iota(jnp.int32, (1, 128), 1) < 64
    below = lax.broadcasted_iota(jnp.int32, (TILE, TILE), 1) <= lax.broadcasted_iota(
        jnp.int32, (TILE, TILE), 0
    )
    vext_ref[:, :128] = v_ref[...]
    vext_ref[:, 128:] = jnp.ones((rows, 128), BF)
    for start in range(0, rows, TILE):
        stop = start + TILE
        both = dot_nt(stacked(q_ref[start:stop], low_lanes), k_ref[:stop])
        peaks, weights = [], []
        for head in range(2):
            raw = both[head * TILE : (head + 1) * TILE]
            parts = []
            if start >= half:
                parts.append((raw[:, :half], cross))
                if start > half:
                    parts.append((raw[:, half:start], None))
            elif start > 0:
                parts.append((raw[:, :start], None))
            parts.append((jnp.where(below, raw[:, start:stop], MASKED), None))
            peak = None
            for piece, shift in parts:
                top = jnp.max(piece, axis=-1, keepdims=True)
                if shift is not None:
                    top = top + shift
                peak = top if peak is None else jnp.maximum(peak, top)
            peaks.append(peak)
            pieces = []
            for piece, shift in parts:
                level = peak if shift is None else peak - shift
                pieces.append(jnp.exp2((piece - level) * factor).astype(BF))
            weights.append(pieces[0] if len(pieces) == 1 else jnp.concatenate(pieces, axis=1))
        both = dot_nn(jnp.concatenate(weights, axis=0), vext_ref[:stop])
        total = jnp.where(low_lanes, both[:TILE, 128:], both[TILE:, 128:])
        peak = jnp.where(low_lanes, peaks[0], peaks[1])
        mixed = jnp.where(low_lanes, both[:TILE, :128], both[TILE:, :128]) / total
        out_ref[start:stop] = mixed
        scaled_ref[start:stop] = (mixed * scale).astype(BF)
        lse = (peak * factor + jnp.log2(total)).T
        lse_ref[0, 0:1, start:stop] = lse[0:1]
        lse_ref[0, 1:2, start:stop] = lse[64:65]


def project_pair(first_ref, weights, bias, proj_ref):
    proj_ref[0] = (dot_nn(first_ref[...], weights) + bias).astype(BF)


def three(proj_ref):
    return [proj_ref.at[0, :, pl.ds(part * 128, 128)] for part in range(3)]


def plain_first_kernel(
    lengths_ref,
    tokens_ref,
    wq_ref,
    wk_ref,
    wv_ref,
    vectors_ref,
    bq_ref,
    bv_ref,
    hs_ref,
    first_ref,
    proj_ref,
    scaled_ref,
    attended_ref,
    lse_ref,
    vext_ref,
):
    @pl.when(pl.program_id(0) == 0)
    def _():
        for start in range(0, tokens_ref.shape[0], TILE):
            rows = pl.ds(start, TILE)
            normed, _ = row_norm(tokens_ref[rows].astype(F32))
            first_ref[rows] = (normed * vectors_ref[3:4] + vectors_ref[4:5]).astype(BF)

    weights = jnp.concatenate([wq_ref[...], wk_ref[...], wv_ref[...]], axis=1)
    bias = jnp.concatenate([bq_ref[0:1], jnp.zeros((1, 128), F32), bv_ref[1:2]], axis=1)
    project_pair(first_ref, weights, bias, proj_ref)
    attention_pair(
        cross_flag(lengths_ref, tokens_ref), *three(proj_ref), hs_ref[...], scaled_ref, attended_ref, lse_ref, vext_ref
    )


def plain_first(lengths, tokens, weights, vectors, head_lanes):
    rows, width = tokens.shape
    pairs = width // 128
    column = pl.BlockSpec((rows, 128), lambda p: (0, p))
    bias = pl.BlockSpec((16, 128), lambda p: (0, p))
    return pl.pallas_call(
        plain_first_kernel,
        grid=(pairs,),
        in_specs=[
            pl.BlockSpec(memory_space=pltpu.SMEM),
            whole((rows, width)),
            pl.BlockSpec((width, 128), lambda p: (0, p)),
            pl.BlockSpec((width, 128), lambda p: (0, pairs + p)),
            pl.BlockSpec((width, 128), lambda p: (0, 2 * pairs + p)),
            whole(vectors.shape),
            bias,
            bias,
            pl.BlockSpec((1, 128), lambda p: (0, p)),
        ],
        out_specs=[
            whole((rows, width)),
            pl.BlockSpec((1, rows, 384), lambda p: (p, 0, 0)),
            column,
            column,
            pl.BlockSpec((1, 8, rows), lambda p: (p, 0, 0)),
        ],
        out_shape=[
            jax.ShapeDtypeStruct((rows, width), BF),
            jax.ShapeDtypeStruct((pairs, rows, 384), BF),
            jax.ShapeDtypeStruct((rows, width), BF),
            jax.ShapeDtypeStruct((rows, width), F32),
            jax.ShapeDtypeStruct((pairs, 8, rows), F32),
        ],
        scratch_shapes=[pltpu.VMEM((rows, 256), BF)],
        compiler_params=params(),
        name="plain_first",
    )(lengths, tokens, weights, weights, weights, vectors, vectors, vectors, head_lanes)


def out_proj_rows(scaled_ref, weight_ref, vec_ref, tokens_ref, branch_ref, middle_ref):
    branch = dot_nn(scaled_ref[...], weight_ref[...]) + vec_ref[2:3]
    normed, _ = row_norm(branch)
    middle = tokens_ref[...].astype(F32) + (normed * vec_ref[5:6] + vec_ref[6:7])
    again, _ = row_norm(middle)
    branch_ref[...] = branch
    middle_ref[...] = middle
    return (again * vec_ref[7:8] + vec_ref[8:9]).astype(BF)


def out_proj_kernel(scaled_ref, weight_ref, vec_ref, tokens_ref, branch_ref, middle_ref, feed_ref):
    feed_ref[...] = out_proj_rows(
        scaled_ref, weight_ref, vec_ref, tokens_ref, branch_ref, middle_ref
    )


def out_proj(scaled, weights, vectors, tokens):
    rows, width = tokens.shape
    by_row = pl.BlockSpec((TILE, width), lambda i: (i, 0))
    return pl.pallas_call(
        out_proj_kernel,
        grid=(rows // TILE,),
        in_specs=[
            by_row,
            whole((width, width)),
            whole(vectors.shape),
            by_row,
        ],
        out_specs=[by_row, by_row, by_row],
        out_shape=[
            jax.ShapeDtypeStruct((rows, width), F32),
            jax.ShapeDtypeStruct((rows, width), F32),
            jax.ShapeDtypeStruct((rows, width), BF),
        ],
        compiler_params=params(),
        name="out_proj",
    )(scaled, weights, vectors, tokens)


def phi_and_slope(value):
    bell = jnp.exp2(value * value * (-0.5 * LOG2E))
    t = 1.0 / (1.0 + (0.3275911 * ROOT_HALF) * jnp.abs(value))
    series = t * (
        0.5 * 0.254829592
        + t
        * (
            0.5 * -0.284496736
            + t * (0.5 * 1.421413741 + t * (0.5 * -1.453152027 + t * (0.5 * 1.061405429)))
        )
    )
    tail = series * bell
    area = jnp.where(value < 0.0, tail, 1.0 - tail)
    return value * area, area + value * bell * INV_ROOT_TAU


def up_step(feed_ref, up, vec, act_ref, slope_ref, sums_ref):
    for left in range(0, UNITS, TILE):
        columns = slice(left, left + TILE)
        pre = dot_nn(feed_ref[...], up[:, columns])
        bias = vec[0:1, columns].astype(F32)
        for start in range(0, feed_ref.shape[0], SLIM):
            rows = slice(start, start + SLIM)
            act, slope = phi_and_slope(pre[rows] + bias)
            act_ref[0, rows, columns] = act.astype(BF)
            slope_ref[0, rows, columns] = slope.astype(BF)
            sums_ref[0, rows] += lane_fold(act)
            sums_ref[1, rows] += lane_fold(act * act)


def side_by_side(*columns):
    lane = lax.broadcasted_iota(jnp.int32, (1, 128), 1)
    result = jnp.broadcast_to(columns[-1], (columns[-1].shape[0], 128))
    for index in range(len(columns) - 2, -1, -1):
        result = jnp.where(lane == index, columns[index], result)
    return result


def up_stats(units, stats_ref, sums_ref):
    for start in range(0, stats_ref.shape[0], TILE):
        rows = pl.ds(start, TILE)
        mean = jnp.sum(sums_ref[0, rows], axis=1, keepdims=True) / units
        square = jnp.sum(sums_ref[1, rows], axis=1, keepdims=True) / units
        inv = lax.rsqrt(square - mean * mean + EPS)
        stats_ref[rows] = side_by_side(mean, inv)


def up_kernel(units, feed_ref, up_ref, vec_ref, act_ref, slope_ref, stats_ref, sums_ref):
    step = pl.program_id(0)

    @pl.when(step == 0)
    def _():
        sums_ref[...] = jnp.zeros_like(sums_ref)

    up_step(feed_ref, up_ref.at[0], vec_ref.at[0], act_ref, slope_ref, sums_ref)

    @pl.when(step == pl.num_programs(0) - 1)
    def _():
        up_stats(units, stats_ref, sums_ref)


def up_pass(feed, up, vec):
    rows, width = feed.shape
    steps = up.shape[0]
    block = pl.BlockSpec((1, rows, UNITS), lambda j: (j, 0, 0))
    return pl.pallas_call(
        functools.partial(up_kernel, steps * UNITS),
        grid=(steps,),
        in_specs=[
            whole((rows, width)),
            pl.BlockSpec((1, width, UNITS), lambda j: (j, 0, 0)),
            pl.BlockSpec((1, vec.shape[1], UNITS), lambda j: (j, 0, 0)),
        ],
        out_specs=[block, block, whole((rows, 128))],
        out_shape=[
            jax.ShapeDtypeStruct((steps, rows, UNITS), BF),
            jax.ShapeDtypeStruct((steps, rows, UNITS), BF),
            jax.ShapeDtypeStruct((rows, 128), F32),
        ],
        scratch_shapes=[pltpu.VMEM((2, rows, 128), F32)],
        compiler_params=params(),
        name="up_pass",
    )(feed, up, vec)


def down_step(
    act_ref, stats_ref, vec, down, cot_ref, down_grad_ref, e_ref, vec_grad_ref, total_ref, sums_ref,
    low_ref
):
    gain = vec[1:2].astype(F32)
    shift = vec[2:3].astype(F32)
    slims = [slice(start, start + SLIM) for start in range(0, cot_ref.shape[0], SLIM)]

    def normalized(rows, columns):
        value = act_ref[0, rows, columns].astype(F32)
        return (value - stats_ref[rows, 0:1]) * stats_ref[rows, 1:2]

    for rows in slims:
        low_ref[rows] = (normalized(rows, slice(0, UNITS)) * gain + shift).astype(BF)
    for left in range(0, UNITS, TILE):
        columns = slice(left, left + TILE)
        grads = dot_nt(cot_ref[...], down[columns])
        gain_grad = jnp.zeros((SLIM, TILE), F32)
        bias_grad = jnp.zeros((SLIM, TILE), F32)
        for rows in slims:
            normed = normalized(rows, columns)
            grad = grads[rows]
            gain_grad = gain_grad + grad * normed
            bias_grad = bias_grad + grad
            e = grad * gain[:, columns]
            e_ref[0, rows, columns] = e.astype(BF)
            sums_ref[0, rows] += lane_fold(e)
            sums_ref[1, rows] += lane_fold(e * normed)
        vec_grad_ref[0, 0:1, columns] = column_sum(gain_grad)
        vec_grad_ref[0, 1:2, columns] = column_sum(bias_grad)
    for left in range(0, total_ref.shape[1], TILE):
        columns = slice(left, left + TILE)
        total_ref[:, columns] += dot_nn(low_ref[...], down[:, columns])
    for left in range(0, UNITS, TILE):
        columns = slice(left, left + TILE)
        down_grad_ref[0, columns] = dot_tn(low_ref[:, columns], cot_ref[...]).astype(BF)


def down_end(
    units, stats_ref, middle_ref, shift_ref, mixed_ref, all_stats_ref, total_ref, sums_ref
):
    for start in range(0, total_ref.shape[0], TILE):
        rows = pl.ds(start, TILE)
        mixed_ref[rows] = (
            middle_ref[rows] + total_ref[rows] + shift_ref[...].astype(F32)
        ).astype(BF)
        first = jnp.sum(sums_ref[0, rows], axis=1, keepdims=True) / units
        cross = jnp.sum(sums_ref[1, rows], axis=1, keepdims=True) / units
        all_stats_ref[rows] = side_by_side(stats_ref[rows, 0:1], stats_ref[rows, 1:2], first, cross)


def down_kernel(
    units,
    act_ref,
    stats_ref,
    vec_ref,
    down_ref,
    cot_ref,
    middle_ref,
    shift_ref,
    mixed_ref,
    down_grad_ref,
    e_ref,
    all_stats_ref,
    vec_grad_ref,
    total_ref,
    sums_ref,
    low_ref,
):
    step = pl.program_id(0)

    @pl.when(step == 0)
    def _():
        total_ref[...] = jnp.zeros_like(total_ref)
        sums_ref[...] = jnp.zeros_like(sums_ref)

    down_step(
        act_ref, stats_ref, vec_ref.at[0], down_ref.at[0], cot_ref, down_grad_ref, e_ref, vec_grad_ref,
        total_ref, sums_ref, low_ref
    )

    @pl.when(step == pl.num_programs(0) - 1)
    def _():
        down_end(
            units, stats_ref, middle_ref, shift_ref, mixed_ref, all_stats_ref, total_ref, sums_ref
        )


def down_pass(act, stats, vec, down, cotangent, middle, shift):
    rows, width = cotangent.shape
    steps = act.shape[0]
    block = pl.BlockSpec((1, rows, UNITS), lambda j: (j, 0, 0))
    return pl.pallas_call(
        functools.partial(down_kernel, steps * UNITS),
        grid=(steps,),
        in_specs=[
            block,
            whole((rows, 128)),
            pl.BlockSpec((1, vec.shape[1], UNITS), lambda j: (j, 0, 0)),
            pl.BlockSpec((1, UNITS, width), lambda j: (j, 0, 0)),
            whole((rows, width)),
            whole((rows, width)),
            whole((1, width)),
        ],
        out_specs=[
            whole((rows, width)),
            pl.BlockSpec((1, UNITS, width), lambda j: (j, 0, 0)),
            block,
            whole((rows, 128)),
            pl.BlockSpec((1, 8, UNITS), lambda j: (j, 0, 0)),
        ],
        out_shape=[
            jax.ShapeDtypeStruct((rows, width), BF),
            jax.ShapeDtypeStruct((steps, UNITS, width), BF),
            jax.ShapeDtypeStruct((steps, rows, UNITS), BF),
            jax.ShapeDtypeStruct((rows, 128), F32),
            jax.ShapeDtypeStruct((steps, 8, UNITS), F32),
        ],
        scratch_shapes=[
            pltpu.VMEM((rows, width), F32),
            pltpu.VMEM((2, rows, 128), F32),
            pltpu.VMEM((rows, UNITS), BF),
        ],
        compiler_params=params(),
        name="down_pass",
    )(act, stats, vec, down, cotangent, middle, shift)


def up_back_step(act, slope, e, stats_ref, up, low_ref, total_ref):
    bias_grad = jnp.zeros((SLIM, UNITS), F32)
    for start in range(0, total_ref.shape[0], SLIM):
        rows = slice(start, start + SLIM)
        inv = stats_ref[rows, 1:2]
        normed = (act[rows].astype(F32) - stats_ref[rows, 0:1]) * inv
        grad_act = inv * (
            e[rows].astype(F32) - stats_ref[rows, 2:3] - normed * stats_ref[rows, 3:4]
        )
        low = (grad_act * slope[rows].astype(F32)).astype(BF)
        bias_grad = bias_grad + low.astype(F32)
        low_ref[rows, 0:UNITS] = low
    for left in range(0, total_ref.shape[1], TILE):
        columns = slice(left, left + TILE)
        total_ref[:, columns] += dot_nt(low_ref[:, 0:UNITS], up[columns])
    return column_sum(bias_grad)


def up_back_kernel(
    act_ref,
    slope_ref,
    e_ref,
    stats_ref,
    up_ref,
    feed_ref,
    up_grad_ref,
    bias_grad_ref,
    total_ref,
    turned_ref,
    low_ref,
):
    @pl.when(pl.program_id(0) == 0)
    def _():
        total_ref[...] = jnp.zeros_like(total_ref)
        turned_ref[...] = feed_ref[...].T

    bias_grad_ref[0, 0:1] = up_back_step(
        act_ref.at[0],
        slope_ref.at[0],
        e_ref.at[0],
        stats_ref,
        up_ref.at[0],
        low_ref,
        total_ref,
    )
    up_grad_ref[0] = dot_nn(turned_ref[...], low_ref[...]).astype(BF)


def up_back(act, slope, e, stats, up, feed):
    rows, width = feed.shape
    steps = act.shape[0]
    block = pl.BlockSpec((1, rows, UNITS), lambda j: (j, 0, 0))
    narrow = whole((rows, 128))
    return pl.pallas_call(
        up_back_kernel,
        grid=(steps,),
        in_specs=[
            block,
            block,
            block,
            narrow,
            pl.BlockSpec((1, width, UNITS), lambda j: (j, 0, 0)),
            whole((rows, width)),
        ],
        out_specs=[
            pl.BlockSpec((1, width, UNITS), lambda j: (j, 0, 0)),
            pl.BlockSpec((1, 8, UNITS), lambda j: (j, 0, 0)),
            whole((rows, width)),
        ],
        out_shape=[
            jax.ShapeDtypeStruct((steps, width, UNITS), BF),
            jax.ShapeDtypeStruct((steps, 8, UNITS), F32),
            jax.ShapeDtypeStruct((rows, width), F32),
        ],
        scratch_shapes=[pltpu.VMEM((width, rows), BF), pltpu.VMEM((rows, UNITS), BF)],
        compiler_params=params(),
        name="up_back",
    )(act, slope, e, stats, up, feed)


def norms_back(grad_feed, cot_ref, middle_ref, branch_ref, vec_ref, sums_ref):
    normed, inv = row_norm(middle_ref[...])
    cot = cot_ref[...].astype(F32)
    grad_middle = cot + norm_back(grad_feed, vec_ref[7:8], normed, inv)
    sums_ref[7:8] += column_sum(grad_feed * normed)
    sums_ref[8:9] += column_sum(grad_feed)
    sums_ref[9:10] += column_sum(cot)
    normed, inv = row_norm(branch_ref[...])
    low = norm_back(grad_middle, vec_ref[5:6], normed, inv).astype(BF)
    sums_ref[5:6] += column_sum(grad_middle * normed)
    sums_ref[6:7] += column_sum(grad_middle)
    sums_ref[2:3] += column_sum(low.astype(F32))
    return grad_middle, low


def heads_back(low, weights, scale, attended):
    grad_out = (dot_nt(low, weights) * scale).astype(BF)
    product = grad_out.astype(F32) * attended
    high = product.astype(BF)
    rest = (product - high.astype(F32)).astype(BF)
    heads = (
        lax.broadcasted_iota(jnp.int32, (product.shape[1], 128), 0) // 64
        == lax.broadcasted_iota(jnp.int32, (product.shape[1], 128), 1)
    ).astype(BF)
    return grad_out, dot_nn(high, heads) + dot_nn(rest, heads)


def out_back_kernel(
    grad_feed_ref,
    cot_ref,
    middle_ref,
    branch_ref,
    scaled_ref,
    attended_ref,
    weight_ref,
    vec_ref,
    hs_ref,
    grad_middle_ref,
    ga_ref,
    out_grad_ref,
    delta_ref,
    sums_ref,
    total_ref,
):
    step = pl.program_id(0)

    @pl.when(step == 0)
    def _():
        total_ref[...] = jnp.zeros_like(total_ref)
        sums_ref[...] = jnp.zeros_like(sums_ref)

    grad_middle, low = norms_back(
        grad_feed_ref[...], cot_ref, middle_ref, branch_ref, vec_ref, sums_ref
    )
    grad_middle_ref[...] = grad_middle
    ga_ref[...], delta = heads_back(low, weight_ref[...], hs_ref[...], attended_ref[...])
    total_ref[...] += dot_tn(scaled_ref[...], low)
    delta_ref[...] = delta.T[: delta_ref.shape[0]]

    @pl.when(step == pl.num_programs(0) - 1)
    def _():
        out_grad_ref[...] = total_ref[...].astype(BF)


def out_back(
    grad_feed, cotangent, middle, branch, scaled, attended, weights, vectors, head_lanes
):
    rows, width = cotangent.shape
    heads = 2 * width // 128
    by_row = pl.BlockSpec((TILE, width), lambda i: (i, 0))
    return pl.pallas_call(
        out_back_kernel,
        grid=(rows // TILE,),
        in_specs=[
            by_row,
            by_row,
            by_row,
            by_row,
            by_row,
            by_row,
            whole((width, width)),
            whole(vectors.shape),
            whole((1, width)),
        ],
        out_specs=[
            by_row,
            by_row,
            whole((width, width)),
            pl.BlockSpec((heads, TILE), lambda i: (0, i)),
            whole((16, width)),
        ],
        out_shape=[
            jax.ShapeDtypeStruct((rows, width), F32),
            jax.ShapeDtypeStruct((rows, width), BF),
            jax.ShapeDtypeStruct((width, width), BF),
            jax.ShapeDtypeStruct((heads, rows), F32),
            jax.ShapeDtypeStruct((16, width), F32),
        ],
        scratch_shapes=[pltpu.VMEM((width, width), F32)],
        compiler_params=params(),
        name="out_back",
    )(
        grad_feed,
        cotangent,
        middle,
        branch,
        scaled,
        attended,
        weights,
        vectors,
        head_lanes,
    )


def attention_back_keys(
    starts, cross, q_ref, k_ref, v_ref, ga_ref, lse_ref, deltas, dq_ref, dk_ref, dv_ref
):
    rows = q_ref.shape[0]
    half = rows // 2
    factor = LOG2E * 64 ** (-0.5)
    low_lanes = lax.broadcasted_iota(jnp.int32, (1, 128), 1) < 64
    above = lax.broadcasted_iota(jnp.int32, (TILE, TILE), 0) <= lax.broadcasted_iota(
        jnp.int32, (TILE, TILE), 1
    )

    def pick(both):
        return jnp.where(low_lanes, both[:TILE], both[TILE:])

    for start in starts:
        stop = start + TILE
        keys = k_ref[start:stop]
        keys_apart = stacked(keys, low_lanes)
        values_apart = stacked(v_ref[start:stop], low_lanes)
        dk = jnp.zeros((TILE, 128), F32)
        dv = jnp.zeros((TILE, 128), F32)
        for left, right in ((start, half), (half, rows)) if start < half else ((start, rows),):
            raw = dot_nt(keys_apart, q_ref[left:right])
            grad_weights = dot_nt(values_apart, ga_ref[left:right])
            weights, grad_scores = [], []
            for head in range(2):
                mine = slice(head * TILE, (head + 1) * TILE)
                level = lse_ref[head : head + 1, left:right]
                if start < half <= left:
                    level = level - cross
                exponent = raw[mine] * factor - level
                if left == start:
                    first = jnp.where(above, exponent[:, :TILE], MASKED)
                    exponent = (
                        first
                        if right - left == TILE
                        else jnp.concatenate([first, exponent[:, TILE:]], axis=1)
                    )
                weight = jnp.exp2(exponent)
                weights.append(weight.astype(BF))
                delta = deltas[head][:, left:right]
                grad_scores.append((weight * (grad_weights[mine] - delta)).astype(BF))
            dv = dv + pick(dot_nn(jnp.concatenate(weights, axis=0), ga_ref[left:right]))
            dk = dk + pick(dot_nn(jnp.concatenate(grad_scores, axis=0), q_ref[left:right]))
            dq = jnp.where(low_lanes, dot_tn(grad_scores[0], keys), dot_tn(grad_scores[1], keys))
            if start == 0:
                dq_ref[left:right] = dq
            else:
                dq_ref[left:right] += dq
        dk_ref[start:stop] = dk
        dv_ref[start:stop] = dv


def in_back_pair(dq_ref, dk_ref, dv_ref, weights, turned_ref, out_grad_ref, chunk_ref, total_ref):
    factor = 64 ** (-0.5)
    dq = (dq_ref[...] * factor).astype(BF)
    dk = (dk_ref[...] * factor).astype(BF)
    dv = dv_ref[...].astype(BF)
    grads = jnp.concatenate([dq, dk, dv], axis=1)
    shares = dot_nn(turned_ref[...], grads).astype(BF)
    for start in range(0, total_ref.shape[0], TILE):
        part = jnp.concatenate(
            [shares[start : start + TILE], out_grad_ref[start : start + TILE]], axis=1
        )
        chunk_ref[:, start // TILE] = part.reshape(8, 32, 512)
        columns = slice(start, start + TILE)
        total_ref[:, columns] += dot_nt(grads, weights[columns])
    return column_sum(dq.astype(F32)), column_sum(dv.astype(F32))


def tokens_back(tokens, grad, grad_middle, gain):
    normed, inv = row_norm(tokens.astype(F32))
    back = norm_back(grad, gain, normed, inv)
    return (grad_middle + back).astype(BF), column_sum(grad * normed), column_sum(grad)


def in_back_kernel(
    lengths_ref,
    proj_ref,
    ga_ref,
    lse_ref,
    delta_ref,
    wq_ref,
    wk_ref,
    wv_ref,
    first_ref,
    out_grad_ref,
    tokens_ref,
    gain_ref,
    grad_middle_ref,
    chunk_ref,
    bias_ref,
    tokens_grad_ref,
    sums_ref,
    dq_ref,
    dk_ref,
    dv_ref,
    turned_ref,
    total_ref,
):
    step = pl.program_id(0)
    q_ref, k_ref, v_ref = three(proj_ref)
    rows_all = tokens_ref.shape[0]

    @pl.when(step == 0)
    def _():
        turned_ref[...] = first_ref[...].T
        total_ref[...] = jnp.zeros_like(total_ref)

    deltas = [delta_ref[0, head : head + 1] for head in range(2)]
    attention_back_keys(
        range(0, rows_all, TILE),
        cross_flag(lengths_ref, tokens_ref),
        q_ref,
        k_ref,
        v_ref,
        ga_ref,
        lse_ref.at[0],
        deltas,
        dq_ref,
        dk_ref,
        dv_ref,
    )
    weights = jnp.concatenate([wq_ref[...], wk_ref[...], wv_ref[...]], axis=1)
    query_sum, value_sum = in_back_pair(
        dq_ref, dk_ref, dv_ref, weights, turned_ref, out_grad_ref, chunk_ref.at[0], total_ref
    )
    bias_ref[0, 0:1] = query_sum
    bias_ref[0, 1:2] = value_sum

    @pl.when(step == pl.num_programs(0) - 1)
    def _():
        gain_grad = jnp.zeros((1, total_ref.shape[1]), F32)
        shift_grad = jnp.zeros((1, total_ref.shape[1]), F32)
        for start in range(0, rows_all, TILE):
            rows = pl.ds(start, TILE)
            tokens_grad_ref[rows], gain_part, shift_part = tokens_back(
                tokens_ref[rows], total_ref[rows], grad_middle_ref[rows], gain_ref[...]
            )
            gain_grad = gain_grad + gain_part
            shift_grad = shift_grad + shift_part
        sums_ref[0:1] = gain_grad
        sums_ref[1:2] = shift_grad


def in_back(lengths, projected, ga, lse, delta, weights, first, out_grad, tokens, gain, grad_middle):
    rows, width = tokens.shape
    pairs = width // 128
    column = pl.BlockSpec((rows, 128), lambda p: (0, p))
    square = whole((rows, width))
    return pl.pallas_call(
        in_back_kernel,
        grid=(pairs,),
        in_specs=[
            pl.BlockSpec(memory_space=pltpu.SMEM),
            pl.BlockSpec((1, rows, 384), lambda p: (p, 0, 0)),
            column,
            pl.BlockSpec((1, 8, rows), lambda p: (p, 0, 0)),
            pl.BlockSpec((1, 2, rows), lambda p: (p, 0, 0)),
            pl.BlockSpec((width, 128), lambda p: (0, p)),
            pl.BlockSpec((width, 128), lambda p: (0, pairs + p)),
            pl.BlockSpec((width, 128), lambda p: (0, 2 * pairs + p)),
            square,
            column,
            square,
            whole((1, width)),
            square,
        ],
        out_specs=[
            pl.BlockSpec((1, 8, width // TILE, 32, 512), lambda p: (p, 0, 0, 0, 0)),
            pl.BlockSpec((1, 8, 128), lambda p: (p, 0, 0)),
            square,
            whole((8, width)),
        ],
        out_shape=[
            jax.ShapeDtypeStruct((pairs, 8, width // TILE, 32, 512), BF),
            jax.ShapeDtypeStruct((pairs, 8, 128), F32),
            jax.ShapeDtypeStruct((rows, width), BF),
            jax.ShapeDtypeStruct((8, width), F32),
        ],
        scratch_shapes=[
            pltpu.VMEM((rows, 128), F32),
            pltpu.VMEM((rows, 128), F32),
            pltpu.VMEM((rows, 128), F32),
            pltpu.VMEM((width, rows), BF),
            pltpu.VMEM((rows, width), F32),
        ],
        compiler_params=params(),
        name="in_back",
    )(
        lengths,
        projected,
        ga,
        lse,
        delta,
        weights,
        weights,
        weights,
        first,
        out_grad,
        tokens,
        gain,
        grad_middle,
    )


class Place:
    def __init__(self):
        self.z = lax.axis_index("dp")
        wide = lax.axis_index("wide")
        self.y = wide // 4
        self.x = (wide // 2) % 2
        self.c = wide % 2
        self.core = (self.z, wide + 1 - 2 * self.c)
        self.side = (self.z, wide + 2 - 4 * self.x)
        self.over = (self.z, wide + 4 - 8 * self.y)
        self.ranks = (self.z + 1 - 2 * (self.z % 2), (self.z + 2) % 4, 3 - self.z)
        self.planes = tuple((rank, wide) for rank in self.ranks)

    def greet(self, planes=True):
        barrier = pltpu.get_barrier_semaphore()
        peers = (self.core, self.side, self.over) + (self.planes if planes else ())
        for peer in peers:
            pl.semaphore_signal(barrier, inc=1, device_id=peer, device_id_type=MESH)
        pl.semaphore_wait(barrier, len(peers))


class WideGather:
    copies = 10

    def __init__(
        self, place, view, count, send, recv, first, source=None, last=None, offset=0, total=None
    ):
        y, x, c = place.y, place.x, place.c
        here, side, over, far = (y, x, c), (y, 1 - x, c), (1 - y, x, c), (1 - y, 1 - x, c)
        upper, lower = pl.ds(offset, count // 2), pl.ds(offset + count // 2, count // 2)
        both = pl.ds(offset, count)
        everything = both if total is None else pl.ds(0, total)

        def copy(index, slot, part, peer):
            destination = view(*slot, part)
            return pltpu.make_async_remote_copy(
                src_ref=source.at[part] if source is not None and slot is here else destination,
                dst_ref=destination,
                send_sem=send.at[first + index],
                recv_sem=recv.at[first + index],
                device_id=peer,
                device_id_type=MESH,
            )

        self.all = (
            copy(0, here, upper, place.side),
            copy(1, here, lower, place.over),
            copy(2, here, upper, place.over),
            copy(3, here, lower, place.side),
            None if total == 0 else copy(4, here, everything, place.core),
            copy(5, side, upper, place.over),
            copy(6, over, lower, place.side),
            copy(7, side, both, place.core),
            copy(8, over, both, place.core),
            copy(9, far, both, place.core),
        )
        self.own = None
        if source is not None and last is not None:
            self.own = pltpu.make_async_copy(source, view(*here, everything), last)

    def start(self):
        if self.own is not None:
            self.own.start()
        for copy in self.all[:5]:
            if copy is not None:
                copy.start()

    def relay(self, stage):
        waits, starts = (((0, 1), (5, 6)), ((2, 3), (7, 8)), ((5, 6), (9,)))[stage]
        for index in waits:
            self.all[index].wait_recv()
        for index in starts:
            self.all[index].start()

    def finish(self):
        for index in (4, 7, 8, 9):
            if self.all[index] is not None:
                self.all[index].wait_recv()
        for copy in self.all:
            if copy is not None:
                copy.wait_send()
        if self.own is not None:
            self.own.wait()


def blocks_of(target):
    return lambda y, x, c, rows: target.at[y, x, c, rows]


LAG = 2


class Reduction:
    slots = 2 * LAG
    deep = 3 * LAG
    keep = 3 * LAG + 2

    @classmethod
    def scratch(cls):
        n, k = cls.slots, cls.keep
        return [
            pltpu.VMEM((cls.deep, 2, 2, 4, 32, 512), BF),
            pltpu.VMEM((n, 2, 2, 4, 32, 512), BF),
            pltpu.VMEM((n, 2, 2, 4, 16, 512), BF),
            pltpu.VMEM((n, 2, 4, 16, 512), BF),
            pltpu.VMEM((n, 4, 32, 512), BF),
            pltpu.VMEM((n, 3, 32, 512), BF),
            pltpu.VMEM((n, 32, 512), BF),
            pltpu.VMEM((k, 3, 32, 512), BF),
            pltpu.SemaphoreType.DMA((6, k)),
            pltpu.SemaphoreType.DMA((6, k)),
            pltpu.SemaphoreType.DMA((cls.deep,)),
        ]

    def __init__(self, place, refs):
        self.place = place
        (
            self.chip,
            self.partner,
            self.first,
            self.second,
            self.plane,
            self.from_z,
            self.sums,
            self.shared,
            self.send,
            self.recv,
            self.local,
        ) = refs

    def copy(self, index, slot, source, target, peer):
        return pltpu.make_async_remote_copy(
            src_ref=source,
            dst_ref=target,
            send_sem=self.send.at[index, slot],
            recv_sem=self.recv.at[index, slot],
            device_id=peer,
            device_id_type=MESH,
        )

    def wait(self, index, slot, arrived):
        self.copy(index, slot, arrived, arrived, self.place.core).wait()

    def load(self, chunk, source):
        slot = chunk % self.deep
        return pltpu.make_async_copy(source, self.chip.at[slot], self.local.at[slot])

    def stage0(self, chunk, view):
        slot, c = chunk % self.slots, self.place.c
        self.copy(
            0, slot, view.at[:, :, 1 - c], self.partner.at[slot], self.place.core
        ).start()
        self.load(chunk, view.at[:, :, c]).start()

    def stage1(self, chunk):
        p, slot, index = self.place, chunk % self.slots, chunk % self.deep
        partner, chip, target = self.partner.at[slot], self.chip.at[index], self.first.at[slot]
        self.load(chunk, partner).wait()
        self.wait(0, slot, partner)
        chip[...] += partner[...]
        self.copy(1, slot, chip.at[:, 1 - p.x, :, pl.ds(0, 16)], target.at[0], p.side).start()
        self.copy(1, slot, chip.at[1 - p.y, :, :, pl.ds(16, 16)], target.at[1], p.over).start()

    def stage2(self, chunk):
        p, slot, index = self.place, chunk % self.slots, chunk % self.deep
        chip, arrived, target = self.chip.at[index], self.first.at[slot], self.second.at[slot]
        self.wait(1, slot, arrived)
        for k in range(2):
            chip[k, p.x, :, 0:16] += arrived[0, k]
            chip[p.y, k, :, 16:32] += arrived[1, k]
        self.copy(2, slot, chip.at[1 - p.y, p.x, :, pl.ds(0, 16)], target.at[0], p.over).start()
        self.copy(2, slot, chip.at[p.y, 1 - p.x, :, pl.ds(16, 16)], target.at[1], p.side).start()

    def stage3(self, chunk):
        p, slot, index = self.place, chunk % self.slots, chunk % self.deep
        arrived, mine, plane = self.second.at[slot], self.chip.at[index, p.y, p.x], self.plane
        self.wait(2, slot, arrived)
        plane[slot, :, 0:16] = mine[:, 0:16] + arrived[0]
        plane[slot, :, 16:32] = mine[:, 16:32] + arrived[1]
        for k in range(3):
            target = self.from_z.at[slot, k]
            self.copy(3, slot, plane.at[slot, p.ranks[k]], target, p.planes[k]).start()

    def stage4(self, chunk):
        slot = chunk % self.slots
        self.wait(3, slot, self.from_z.at[slot])
        total = self.plane[slot, self.place.z].astype(F32)
        for k in range(3):
            total = total + self.from_z[slot, k].astype(F32)
        return total

    def spread(self, chunk, total):
        slot, place = chunk % self.slots, chunk % self.keep
        self.sums[slot] = total.astype(BF)
        peer = self.place.planes[1]
        self.copy(4, place, self.sums.at[slot], self.shared.at[place, 0], peer).start()

    def stage5(self, chunk):
        slot, place, peer = chunk % self.slots, chunk % self.keep, self.place.planes[0]
        shared = self.shared.at[place]
        self.wait(4, place, shared.at[0])
        self.copy(5, place, self.sums.at[slot], shared.at[1], peer).start()
        self.copy(5, place, shared.at[0], shared.at[2], peer).start()

    def stage6(self, chunk):
        slot, place, ranks = chunk % self.slots, chunk % self.keep, self.place.ranks
        self.wait(5, place, self.shared.at[place, pl.ds(1, 2)])
        return [
            (self.place.z, self.sums[slot]),
            (ranks[1], self.shared[place, 0]),
            (ranks[0], self.shared[place, 1]),
            (ranks[2], self.shared[place, 2]),
        ]


class SmallReduction:
    @staticmethod
    def scratch():
        return [
            pltpu.VMEM((2, 2, 2, 4, 16, 512), BF),
            pltpu.VMEM((2, 2, 4, 16, 512), BF),
            pltpu.VMEM((2, 2, 4, 16, 512), BF),
            pltpu.VMEM((2, 4, 16, 512), BF),
            pltpu.VMEM((4, 16, 512), BF),
            pltpu.VMEM((3, 16, 512), BF),
            pltpu.SemaphoreType.DMA((4,)),
            pltpu.SemaphoreType.DMA((4,)),
        ]

    def __init__(self, place, refs):
        self.place = place
        self.source, self.chip, self.partner, self.first, self.second, self.from_z = refs[:6]
        self.send, self.recv = refs[6:]

    def copy(self, index, source, target, peer):
        return pltpu.make_async_remote_copy(
            src_ref=source,
            dst_ref=target,
            send_sem=self.send.at[index],
            recv_sem=self.recv.at[index],
            device_id=peer,
            device_id_type=MESH,
        )

    def wait(self, index, arrived):
        self.copy(index, arrived, arrived, self.place.core).wait()

    def stage0(self):
        p = self.place
        self.copy(0, self.source.at[:, :, 1 - p.c], self.partner, p.core).start()

    def stage1(self):
        p = self.place
        self.wait(0, self.partner)
        self.chip[...] = self.source[:, :, p.c] + self.partner[...]
        self.copy(1, self.chip.at[:, 1 - p.x], self.first, p.side).start()

    def stage2(self):
        p = self.place
        self.wait(1, self.first)
        for k in range(2):
            self.chip[k, p.x] += self.first[k]
        self.copy(2, self.chip.at[1 - p.y, p.x], self.second, p.over).start()

    def stage3(self):
        p = self.place
        self.wait(2, self.second)
        self.chip[p.y, p.x] += self.second[...]
        for k in range(3):
            block = self.chip.at[p.y, p.x, p.ranks[k]]
            self.copy(3, block, self.from_z.at[k], p.planes[k]).start()

    def stage4(self):
        p = self.place
        self.wait(3, self.from_z)
        total = self.chip[p.y, p.x, p.z].astype(F32)
        for k in range(3):
            total = total + self.from_z[k].astype(F32)
        return total


class Stream:
    def __init__(self, view, buffers, sems):
        self.view, self.buffers, self.sems = view, buffers, sems

    def copy(self, index):
        slot = index % 2
        return pltpu.make_async_copy(self.view(index), self.buffers.at[slot], self.sems.at[slot])

    def start(self, index):
        self.copy(index).start()

    def block(self, index):
        return self.buffers.at[index % 2]


def advance(streams, index, count):
    @pl.when(index + 1 < count)
    def _():
        for stream in streams:
            stream.start(index + 1)

    for stream in streams:
        stream.copy(index).wait()


def nearness(i):
    over = (i == 3) | (i >= 5)
    side = (i == 2) | (i == 4) | (i >= 6)
    other = (i == 1) | (i == 4) | (i == 5) | (i == 7)
    return over, side, other


def unit_index(i):
    wide = lax.axis_index("wide")
    y, x, c = wide // 4, wide // 2 % 2, wide % 2
    over, side, other = nearness(i)
    y, x, c = (jnp.where(flip, 1 - k, k) for flip, k in zip((over, side, other), (y, x, c)))
    return 4 * y + 2 * x + c


class NearGather:
    copies = 3

    def __init__(self, place, source, target, send, recv, first, last):
        slot = target.at[place.y, place.x, place.c]
        self.all = [
            pltpu.make_async_remote_copy(
                src_ref=source,
                dst_ref=slot,
                send_sem=send.at[first + index],
                recv_sem=recv.at[first + index],
                device_id=peer,
                device_id_type=MESH,
            )
            for index, peer in enumerate((place.side, place.over, place.core))
        ]
        self.own = pltpu.make_async_copy(source, slot, last)

    def start(self):
        self.own.start()
        for copy in self.all:
            copy.start()

    def finish(self):
        self.own.wait()
        for copy in self.all:
            copy.wait()


class LateGather:
    copies = 5

    def __init__(self, place, near, late, send, recv, first):
        rows = near.shape[-2]
        upper, lower = pl.ds(0, rows // 2), pl.ds(rows // 2, rows // 2)
        side, over = near.at[place.y, 1 - place.x, place.c], near.at[1 - place.y, place.x, place.c]

        def copy(index, source, target, peer):
            return pltpu.make_async_remote_copy(
                src_ref=source,
                dst_ref=target,
                send_sem=send.at[first + index],
                recv_sem=recv.at[first + index],
                device_id=peer,
                device_id_type=MESH,
            )

        self.all = (
            copy(0, side.at[upper], late.at[2, upper], place.over),
            copy(1, over.at[lower], late.at[2, lower], place.side),
            copy(2, side, late.at[0], place.core),
            copy(3, over, late.at[1], place.core),
            copy(4, late.at[2], late.at[3], place.core),
        )

    def start(self):
        for copy in self.all[:4]:
            copy.start()

    def relay(self):
        for copy in self.all[:2]:
            copy.wait_recv()
        self.all[4].start()

    def arrived(self, *indices):
        for index in indices:
            self.all[index].wait_recv()

    def finish(self):
        for copy in self.all:
            copy.wait_send()


class WeightStream(Stream):
    def __init__(self, near, late, buffers, sems):
        super().__init__(lambda i: late.at[0], buffers, sems)
        self.near, self.late = near, late

    def start(self, index):
        slot = index % 2
        target, sem = self.buffers.at[slot], self.sems.at[slot]

        @pl.when(index < 4)
        def _():
            block = unit_index(index)
            view = self.near.at[block // 4, block // 2 % 2, block % 2]
            pltpu.make_async_copy(view, target, sem).start()

        @pl.when(index >= 4)
        def _():
            pltpu.make_async_copy(self.late.at[index - 4], target, sem).start()


def dma_sems(count):
    return [pltpu.SemaphoreType.DMA((count,)), pltpu.SemaphoreType.DMA((count,))]


def to_planes(place, mine, landing, send, recv, first):
    return [
        pltpu.make_async_remote_copy(
            src_ref=mine,
            dst_ref=landing(k),
            send_sem=send.at[first + k],
            recv_sem=recv.at[first + k],
            device_id=place.planes[k],
            device_id_type=MESH,
        )
        for k in range(3)
    ]


class PlanesLast:
    copies = WideGather.copies + 6

    def __init__(self, place, source, target, send, recv, last):
        view = blocks_of(target.at[place.z])
        self.wide = WideGather(place, view, source.shape[0], send, recv, 0, source, last)

        def copy(index, rank, peer):
            blocks = target.at[rank, :, :, place.c]
            return pltpu.make_async_remote_copy(
                src_ref=blocks,
                dst_ref=blocks,
                send_sem=send.at[WideGather.copies + index],
                recv_sem=recv.at[WideGather.copies + index],
                device_id=peer,
                device_id_type=MESH,
            )

        self.across = [copy(k, place.z, place.planes[k]) for k in range(3)]
        self.over = [copy(3 + k, place.ranks[k], place.core) for k in range(3)]

    def start_across(self):
        self.wide.own.wait()
        for copy in self.across:
            copy.start()

    def start_over(self):
        for arrived, copy in zip(self.across, self.over):
            arrived.wait_recv()
            copy.start()

    def finish(self):
        self.wide.own = None
        self.wide.finish()
        for copy in self.across:
            copy.wait_send()
        for copy in self.over:
            copy.wait()


def first_kernel(
    lengths_ref,
    tokens_ref,
    in_ref,
    vec_ref,
    out_ref,
    up_ref,
    unit_ref,
    hs_ref,
    turned_ref,
    proj_ref,
    scaled_ref,
    scaled_turned_ref,
    attended_ref,
    lse_ref,
    vectors_ref,
    scale_ref,
    in_all,
    out_all,
    up_all,
    unit_all,
    held_ref,
    normed_ref,
    first_ref,
    vext_ref,
    send_in,
    recv_in,
    send_out,
    recv_out,
    send_ff,
    recv_ff,
    local,
):
    step = pl.program_id(0)
    place = Place()
    width = tokens_ref.shape[1]
    count = WideGather.copies
    lanes = (3 * width // 2 + 128, 3 * width // 2)
    across, early, late = [], [], None
    for group in range(2):
        held = held_ref.at[group, :, :, :, :, :, pl.ds(0, lanes[group])]
        first = group * (3 + 2 * count)

        def blocks(planes, held=held):
            return lambda y, x, c, rows: held.at[planes, y, x, c, rows]

        mine = held.at[0, place.y, place.x, place.c]
        across.append(
            to_planes(
                place,
                mine,
                lambda k, held=held: held.at[k + 1, place.y, place.x, place.c],
                send_in,
                recv_in,
                first,
            )
        )
        if group == 0:
            for part, planes in enumerate((pl.ds(0, 1), pl.ds(1, 3))):
                start = first + 3 + part * count
                early.append(WideGather(place, blocks(planes), 32, send_in, recv_in, start))
        else:
            late = WideGather(place, blocks(pl.ds(0, 4)), 32, send_in, recv_in, first + 3)
    orders = (place.z, *place.ranks)
    out = PlanesLast(place, out_ref, out_all, send_out, recv_out, local.at[2])
    up = NearGather(place, up_ref, up_all, send_ff, recv_ff, count, local.at[3])
    unit = WideGather(
        place, blocks_of(unit_all), 32, send_ff, recv_ff, 0, unit_ref, local.at[4]
    )
    keep = [
        pltpu.make_async_copy(
            held_ref.at[group, index, :, :, :, :, pl.ds(0, lanes[1])],
            in_all.at[rank, :, :, :, :, pl.ds(group * lanes[1], lanes[1])],
            local.at[12 + 4 * group + index],
        )
        for group in range(2)
        for index, rank in enumerate(orders)
    ]

    @pl.when(step == 0)
    def _():
        place.greet()
        half = width // 2
        for group in range(2):
            mine = held_ref.at[group, 0, place.y, place.x, place.c]
            fills = []
            for pair in range(4):
                for part in range(3):
                    column = part * width + (4 * group + pair) * 128
                    fills.append(
                        pltpu.make_async_copy(
                            in_ref.at[:, pl.ds(column, 128)],
                            mine.at[:, pl.ds(pair * 384 + part * 128, 128)],
                            local.at[20 + group * 12 + pair * 3 + part],
                        )
                    )
            for copy in fills:
                copy.start()
            if group == 0:
                mine[:, 3 * half : 3 * half + 128] = jnp.zeros((32, 128), BF)
                mine[:, 3 * half : 3 * half + 32] = vec_ref[...]
            for copy in fills:
                copy.wait()
            for copy in across[group]:
                copy.start()
            if group == 0:
                early[0].start()
        scale = hs_ref[...].astype(F32)
        for pair in range(width // 128):
            own = slice(pair * 128, (pair + 1) * 128)
            low_lanes = lax.broadcasted_iota(jnp.int32, (1, 128), 1) < 64
            scale_ref[0:1, own] = jnp.where(
                low_lanes, scale[:, 2 * pair : 2 * pair + 1], scale[:, 2 * pair + 1 : 2 * pair + 2]
            )
        for start in range(0, tokens_ref.shape[0], TILE):
            rows = pl.ds(start, TILE)
            normed, _ = row_norm(tokens_ref[rows].astype(F32))
            normed_ref[rows] = normed
        early[0].relay(0)
        for copy in across[0]:
            copy.wait_recv()
        early[1].start()
        early[0].relay(1)
        early[0].relay(2)
        early[1].relay(0)
        early[1].relay(1)
        for copy in across[1]:
            copy.wait_recv()
        late.start()
        early[1].relay(2)
        out.wide.start()
        unit.start()
        for part in early:
            part.finish()
        for z in range(4):
            for y in range(2):
                tile = jnp.zeros((16, 128), F32)
                for x in range(2):
                    for c in range(2):
                        piece = held_ref[
                            0, orders[z], y, x, c, 0:16, 3 * half : 3 * half + 128
                        ].astype(F32)
                        spot = 32 * (2 * x + c)
                        tile = tile + (piece if spot == 0 else pltpu.roll(piece, spot, 1))
                vectors_ref[:, (2 * z + y) * 128 : (2 * z + y + 1) * 128] = tile
        for start in range(0, tokens_ref.shape[0], TILE):
            rows = pl.ds(start, TILE)
            first_ref[rows] = (normed_ref[rows] * vectors_ref[3:4] + vectors_ref[4:5]).astype(BF)

    @pl.when((step >= 2) & (step <= 4))
    def _():
        for stage in range(3):

            @pl.when(step == 2 + stage)
            def _():
                late.relay(stage)
                out.wide.relay(stage)
                unit.relay(stage)

    @pl.when(step == 2)
    def _():
        up.start()

    @pl.when(step == 4)
    def _():
        out.start_across()

    @pl.when(step == 5)
    def _():
        late.finish()
        for copy in keep:
            copy.start()

    @pl.when(step == 7)
    def _():
        out.start_over()

    @pl.when(step > 0)
    def _():
        pair = step - 1
        columns = pl.ds(pl.multiple_of(pair % 4 * 384, 128), 384)
        weights = jnp.concatenate(
            [held_ref[pair // 4, order, :, :, :, :, columns].reshape(TILE, 384) for order in orders]
        )
        own = pl.ds(pl.multiple_of(pair * 128, 128), 128)
        bias = jnp.concatenate(
            [vectors_ref[0:1, own], jnp.zeros((1, 128), F32), vectors_ref[1:2, own]], axis=1
        )
        project_pair(first_ref, weights, bias, proj_ref)
        attention_pair(
            cross_flag(lengths_ref, tokens_ref),
            *three(proj_ref),
            scale_ref[0:1, own],
            scaled_ref,
            attended_ref,
            lse_ref,
            vext_ref,
        )
        scaled_turned_ref[...] = scaled_ref[...].T

    @pl.when(step == pl.num_programs(0) - 1)
    def _():
        turned_ref[...] = first_ref[...].T
        for copy in (*across[0], *across[1]):
            copy.wait_send()
        for copy in keep:
            copy.wait()
        out.finish()
        unit.finish()
        up.finish()


def first_part(lengths, tokens, in_weight, vec, out_weight, up_weight, unit_rows, head_scale):
    rows, width = tokens.shape
    pairs = width // 128

    def at(step):
        return jnp.maximum(step - 1, 0)

    column = pl.BlockSpec((rows, 128), lambda s: (0, at(s)))
    held = (2, 4, 2, 2, 2, 32, 3 * width // 2 + 128)
    return pl.pallas_call(
        first_kernel,
        grid=(pairs + 1,),
        in_specs=[
            pl.BlockSpec(memory_space=pltpu.SMEM),
            whole((rows, width)),
            ANY,
            whole(vec.shape),
            ANY,
            ANY,
            ANY,
            whole(head_scale.shape),
        ],
        out_specs=[
            whole((width, rows)),
            pl.BlockSpec((1, rows, 384), lambda s: (at(s), 0, 0)),
            column,
            pl.BlockSpec((128, rows), lambda s: (at(s), 0)),
            column,
            pl.BlockSpec((1, 8, rows), lambda s: (at(s), 0, 0)),
            whole((16, width)),
            whole((8, width)),
            ANY,
            ANY,
            ANY,
            ANY,
        ],
        out_shape=[
            jax.ShapeDtypeStruct((width, rows), BF),
            jax.ShapeDtypeStruct((pairs, rows, 384), BF),
            jax.ShapeDtypeStruct((rows, width), BF),
            jax.ShapeDtypeStruct((width, rows), BF),
            jax.ShapeDtypeStruct((rows, width), F32),
            jax.ShapeDtypeStruct((pairs, 8, rows), F32),
            jax.ShapeDtypeStruct((16, width), F32),
            jax.ShapeDtypeStruct((8, width), F32),
            jax.ShapeDtypeStruct((4, 2, 2, 2, 32, 3 * width), BF),
            jax.ShapeDtypeStruct((4, 2, 2, 2, *out_weight.shape), BF),
            jax.ShapeDtypeStruct((2, 2, 2, *up_weight.shape), BF),
            jax.ShapeDtypeStruct((2, 2, 2, *unit_rows.shape), BF),
        ],
        scratch_shapes=[
            pltpu.VMEM(held, BF),
            pltpu.VMEM((rows, width), F32),
            pltpu.VMEM((rows, width), BF),
            pltpu.VMEM((rows, 256), BF),
            *dma_sems(6 + 3 * WideGather.copies),
            *dma_sems(PlanesLast.copies),
            *dma_sems(WideGather.copies + NearGather.copies),
            pltpu.SemaphoreType.DMA((44,)),
        ],
        compiler_params=params(collective_id=0, has_side_effects=True),
        name="first_part",
    )(lengths, tokens, in_weight, vec, out_weight, up_weight, unit_rows, head_scale)


def second_kernel(
    units,
    scaled_ref,
    weight_ref,
    vec_ref,
    tokens_ref,
    unit_ref,
    up_near,
    down_ref,
    branch_ref,
    middle_ref,
    turned_ref,
    act_ref,
    slope_ref,
    stats_ref,
    up_late,
    down_near,
    feed_ref,
    sums_ref,
    up_ref,
    send,
    recv,
    local,
    stream_sems,
):
    step = pl.program_id(0)
    lead = feed_ref.shape[0] // TILE
    place = Place()
    late = LateGather(place, up_near, up_late, send, recv, 0)
    down = NearGather(place, down_ref, down_near, send, recv, LateGather.copies, local.at[0])
    up = WeightStream(up_near, up_late, up_ref, stream_sems)

    @pl.when(step == 0)
    def _():
        place.greet(planes=False)
        late.start()
        up.start(0)
        sums_ref[...] = jnp.zeros_like(sums_ref)

    @pl.when(step == 2)
    def _():
        down.start()

    @pl.when(step < lead)
    def _():
        rows = pl.ds(pl.multiple_of(step * TILE, TILE), TILE)
        feed_ref[rows] = out_proj_rows(
            scaled_ref, weight_ref, vec_ref, tokens_ref, branch_ref, middle_ref
        )

    @pl.when(step >= lead)
    def _():
        block = step - lead

        @pl.when(block == 2)
        def _():
            late.relay()

        @pl.when(block == 3)
        def _():
            late.arrived(2, 3)

        @pl.when(block == 6)
        def _():
            late.arrived(4)

        advance((up,), block, 8)
        up_step(feed_ref, up.block(block), unit_ref.at[0], act_ref, slope_ref, sums_ref)

    @pl.when(step == pl.num_programs(0) - 1)
    def _():
        up_stats(units, stats_ref, sums_ref)
        turned_ref[...] = feed_ref[...].T
        late.finish()
        down.finish()


def second_part(scaled, out_weights, vectors, tokens, up_near, unit_vec, down_weight):
    rows, width = tokens.shape
    steps = 8
    lead = rows // TILE

    def early(step):
        return jnp.minimum(step, lead - 1)

    def unit(step):
        return unit_index(jnp.maximum(step - lead, 0))

    by_row = pl.BlockSpec((TILE, width), lambda s: (early(s), 0))
    block = pl.BlockSpec((1, rows, UNITS), lambda s: (unit(s), 0, 0))
    return pl.pallas_call(
        functools.partial(second_kernel, steps * UNITS),
        grid=(lead + steps,),
        in_specs=[
            by_row,
            whole((width, width)),
            whole(vectors.shape),
            by_row,
            pl.BlockSpec((1, unit_vec.shape[1], UNITS), lambda s: (unit(s), 0, 0)),
            ANY,
            ANY,
        ],
        out_specs=[
            by_row,
            by_row,
            whole((width, rows)),
            block,
            block,
            whole((rows, 128)),
            ANY,
            ANY,
        ],
        out_shape=[
            jax.ShapeDtypeStruct((rows, width), F32),
            jax.ShapeDtypeStruct((rows, width), F32),
            jax.ShapeDtypeStruct((width, rows), BF),
            jax.ShapeDtypeStruct((steps, rows, UNITS), BF),
            jax.ShapeDtypeStruct((steps, rows, UNITS), BF),
            jax.ShapeDtypeStruct((rows, 128), F32),
            jax.ShapeDtypeStruct((4, *up_near.shape[3:]), BF),
            jax.ShapeDtypeStruct((2, 2, 2, *down_weight.shape), BF),
        ],
        scratch_shapes=[
            pltpu.VMEM((rows, width), BF),
            pltpu.VMEM((2, rows, 128), F32),
            pltpu.VMEM((2, *up_near.shape[3:]), BF),
            *dma_sems(LateGather.copies + NearGather.copies),
            pltpu.SemaphoreType.DMA((1,)),
            pltpu.SemaphoreType.DMA((2,)),
        ],
        compiler_params=params(collective_id=2, has_side_effects=True),
        name="second_part",
    )(scaled, out_weights, vectors, tokens, unit_vec, up_near, down_weight)


def third_kernel(
    units,
    act_ref,
    stats_ref,
    vec_ref,
    cot_ref,
    middle_ref,
    shift_ref,
    down_near,
    mixed_ref,
    down_grad_ref,
    e_ref,
    all_stats_ref,
    vec_grad_ref,
    down_late,
    total_ref,
    sums_ref,
    low_ref,
    down_ref,
    send,
    recv,
    stream_sems,
):
    step = pl.program_id(0)
    place = Place()
    late = LateGather(place, down_near, down_late, send, recv, 0)
    down = WeightStream(down_near, down_late, down_ref, stream_sems)

    @pl.when(step == 0)
    def _():
        place.greet(planes=False)
        late.start()
        down.start(0)
        total_ref[...] = jnp.zeros_like(total_ref)
        sums_ref[...] = jnp.zeros_like(sums_ref)

    @pl.when(step == 3)
    def _():
        late.relay()
        late.arrived(2, 3)

    @pl.when(step == 6)
    def _():
        late.arrived(4)

    advance((down,), step, 8)
    down_step(
        act_ref, stats_ref, vec_ref.at[0], down.block(step), cot_ref, down_grad_ref, e_ref,
        vec_grad_ref, total_ref, sums_ref, low_ref
    )

    @pl.when(step == pl.num_programs(0) - 1)
    def _():
        down_end(
            units, stats_ref, middle_ref, shift_ref, mixed_ref, all_stats_ref, total_ref, sums_ref
        )
        late.finish()


def third_part(act, stats, vec, down_near, cotangent, middle, shift):
    rows, width = cotangent.shape
    steps = 8

    def unit(shape):
        return pl.BlockSpec((1, *shape), lambda s: (unit_index(s), 0, 0))

    block = unit((rows, UNITS))
    return pl.pallas_call(
        functools.partial(third_kernel, steps * UNITS),
        grid=(steps,),
        in_specs=[
            block,
            whole((rows, 128)),
            unit((vec.shape[1], UNITS)),
            whole((rows, width)),
            whole((rows, width)),
            whole((1, width)),
            ANY,
        ],
        out_specs=[
            whole((rows, width)),
            unit((UNITS, width)),
            block,
            whole((rows, 128)),
            unit((8, UNITS)),
            ANY,
        ],
        out_shape=[
            jax.ShapeDtypeStruct((rows, width), BF),
            jax.ShapeDtypeStruct((steps, UNITS, width), BF),
            jax.ShapeDtypeStruct((steps, rows, UNITS), BF),
            jax.ShapeDtypeStruct((rows, 128), F32),
            jax.ShapeDtypeStruct((steps, 8, UNITS), F32),
            jax.ShapeDtypeStruct((4, *down_near.shape[3:]), BF),
        ],
        scratch_shapes=[
            pltpu.VMEM((rows, width), F32),
            pltpu.VMEM((2, rows, 128), F32),
            pltpu.VMEM((rows, UNITS), BF),
            pltpu.VMEM((2, *down_near.shape[3:]), BF),
            *dma_sems(LateGather.copies),
            pltpu.SemaphoreType.DMA((2,)),
        ],
        compiler_params=params(collective_id=3, has_side_effects=True),
        name="third_part",
    )(act, stats, vec, cotangent, middle, shift, down_near)


NORMS_AT, COLUMNS_AT, HEADS_AT, TOKENS_AT, VECTORS_AT = 8, 16, 20, 28, 32
BACK_STEPS = VECTORS_AT + 7
OUT_TILE = 128


def chunk_at(time):
    chunk = jnp.where(time < 13, time, time - 1)
    chunk = jnp.where(time >= 20, (time + 17) // 2, chunk)
    return chunk, (time >= 0) & ((time < 13) | ((time >= 14) & (time < 20)) | ((time >= 20) & (time < 30) & (time % 2 == 1)))


def back_kernel(
    lengths_ref,
    unit_grad_ref,
    vec_ref,
    hs_ref,
    act_all,
    slope_all,
    e_all,
    stats_all,
    up_near,
    up_late,
    feed_turned_all,
    down_grad_all,
    cot_all,
    middle_all,
    branch_all,
    scaled_turned_all,
    attended_all,
    out_weight_all,
    proj_all,
    lse_all,
    in_weight_all,
    turned_all,
    tokens_all,
    down_out,
    up_out,
    in_out,
    out_out,
    vec_out,
    tokens_grad_all,
    up_grad_all,
    units_in_ref,
    up_ref,
    stats_ref,
    feed_turned_ref,
    cot_ref,
    norms_in_ref,
    scaled_turned_ref,
    attended_ref,
    out_weight_ref,
    proj_ref,
    lse_ref,
    in_weight_ref,
    turned_ref,
    tokens_ref,
    tokens_grad_ref,
    staged_ref,
    total_ref,
    low_ref,
    out_grad_ref,
    ga_ref,
    grad_middle_ref,
    delta_ref,
    delta_sum_ref,
    sums_ref,
    units_ref,
    dq_ref,
    dk_ref,
    dv_ref,
    chunk_ref,
    stream_sems,
    fetch_sems,
    *scratch,
):
    step = pl.program_id(0)
    place = Place()
    engine = Reduction(place, scratch[:11])
    small = SmallReduction(place, scratch[11:])
    pairs = proj_all.shape[0]

    def rows_of(array, size):
        return lambda i: array.at[pl.ds(pl.multiple_of(i * size, size), size)]

    def columns_of(array, size):
        return lambda i: array.at[:, pl.ds(pl.multiple_of(i * size, size), size)]

    def stream(number, view, buffers):
        return Stream(view, buffers, stream_sems.at[number])

    act, slope, e = (
        stream(k, lambda i, array=array: array.at[unit_index(i)], units_in_ref.at[k])
        for k, array in enumerate((act_all, slope_all, e_all))
    )
    up = WeightStream(up_near, up_late, up_ref, stream_sems.at[3])
    cot = stream(4, rows_of(cot_all, OUT_TILE), cot_ref)
    middle = stream(5, rows_of(middle_all, OUT_TILE), norms_in_ref.at[0])
    branch = stream(6, rows_of(branch_all, OUT_TILE), norms_in_ref.at[1])
    attended = stream(7, columns_of(attended_all, TILE), attended_ref)
    proj = stream(8, lambda i: proj_all.at[i], proj_ref)
    lse = stream(9, lambda i: lse_all.at[i], lse_ref)
    in_weight = stream(10, columns_of(in_weight_all, 384), in_weight_ref)
    tokens = stream(11, rows_of(tokens_all, TILE), tokens_ref)
    put = rows_of(tokens_grad_all, TILE)

    def put_tokens(i):
        return pltpu.make_async_copy(
            tokens_grad_ref.at[i % 2], put(i), stream_sems.at[12, i % 2]
        )

    fetches = [
        pltpu.make_async_copy(source, target, fetch_sems.at[index])
        for index, (source, target) in enumerate(
            (
                (stats_all, stats_ref),
                (feed_turned_all, feed_turned_ref),
                (scaled_turned_all, scaled_turned_ref),
                (out_weight_all, out_weight_ref),
                (turned_all, turned_ref),
            )
        )
    ]

    @pl.when(step == 0)
    def _():
        for item in (act, slope, e, up):
            item.start(0)
        for copy in fetches:
            copy.start()
        for item in (cot, middle, branch, attended, proj, lse, in_weight, tokens):
            item.copy(0).start()
        total_ref[...] = jnp.zeros_like(total_ref)
        sums_ref[...] = jnp.zeros_like(sums_ref)
        units_ref[...] = jnp.zeros_like(units_ref)
        place.greet()

    def store(index):
        block = unit_index(index)
        view = up_grad_all.at[block // 4, block // 2 % 2, block % 2]
        return pltpu.make_async_copy(staged_ref, view, fetch_sems.at[5])

    @pl.when((step >= 1) & (step <= NORMS_AT))
    def _():
        store(step - 1).wait()


    def stage(number, kind, action, tick):
        chunk, there = chunk_at(tick - number * LAG)
        up = ((chunk >= 8) & (chunk < 14)) | (chunk == 15) | (chunk == 17)
        wanted = {
            "all": there,
            "down": there & (chunk < 8),
            "up": there & up,
            "shared": there & ((chunk < 8) | up),
            "own": there & (chunk >= 8) & ~up,
        }

        @pl.when(wanted[kind])
        def _():
            action(chunk)

    def up_index(chunk):
        return jnp.where(chunk < 14, chunk - 8, (chunk - 3) // 2)

    def pair_index(chunk):
        return jnp.where(chunk < 18, (chunk - 14) // 2, chunk - 16)

    def put_down(chunk):
        for rank, block in engine.stage6(chunk):
            for half in range(2):

                @pl.when(chunk % 2 == half)
                def _():
                    down_out[chunk // 2, rank, :, half * 512 : half * 512 + 512] = block

    def put_up(chunk):
        for rank, block in engine.stage6(chunk):
            up_out[up_index(chunk), rank] = block

    def put_own(chunk):
        total = engine.stage4(chunk)
        first = pair_index(chunk) * 128
        for part in range(3):
            lanes = pl.ds(pl.multiple_of(part * 1024 + first, 128), 128)
            in_out[:, lanes] = total[:, part * 128 : part * 128 + 128]
        out_out[:, pl.ds(pl.multiple_of(first, 128), 128)] = total[:, 384:512]

    def take_down(chunk):
        lanes = pl.ds(pl.multiple_of(chunk % 2 * 512, 512), 512)
        engine.stage0(chunk, down_grad_all.at[:, :, :, chunk // 2, :, :, lanes])

    def take_up(chunk):
        engine.stage0(chunk, up_grad_all.at[:, :, :, up_index(chunk)])

    def take_own(chunk):
        engine.stage0(chunk, chunk_ref.at[pair_index(chunk) % 2])

    def reduce_step(tick):
        stage(6, "down", put_down, tick)
        stage(6, "up", put_up, tick)
        stage(5, "shared", engine.stage5, tick)
        stage(4, "shared", lambda chunk: engine.spread(chunk, engine.stage4(chunk)), tick)
        stage(4, "own", put_own, tick)
        stage(3, "all", engine.stage3, tick)
        stage(2, "all", engine.stage2, tick)
        stage(1, "all", engine.stage1, tick)
        stage(0, "down", take_down, tick)
        stage(0, "up", take_up, tick)

    tick = jnp.where(step < NORMS_AT, step, NORMS_AT + (step - NORMS_AT) // 4)
    tick = jnp.where(step < COLUMNS_AT, tick, step - 6)
    tick = jnp.where(step < HEADS_AT, tick, 2 * step - 26)
    tick = jnp.where(step < TOKENS_AT, tick, 30)
    tick = jnp.where(step < VECTORS_AT, tick, step - 1)
    within = (step > NORMS_AT) & (step < COLUMNS_AT) & (step % 4 != 0)
    within = within | ((step > TOKENS_AT) & (step < VECTORS_AT))

    @pl.when(~within)
    def _():
        reduce_step(tick)


    @pl.when(step < NORMS_AT)
    def _():
        advance((act, slope, e, up), step, NORMS_AT)

        @pl.when(step == 0)
        def _():
            fetches[0].wait()

        unit = unit_index(step)
        units_ref[unit, 0:1] = up_back_step(
            act.block(step),
            slope.block(step),
            e.block(step),
            stats_ref,
            up.block(step),
            low_ref,
            total_ref,
        )
        units_ref[unit, 1:3] = unit_grad_ref[unit, 0:2]

        @pl.when(step == 0)
        def _():
            fetches[1].wait()

        for left in range(0, UNITS, TILE):
            columns = slice(left, left + TILE)
            grad = dot_nn(feed_turned_ref[...], low_ref[:, columns]).astype(BF)
            staged_ref[:, :, :, columns] = grad.reshape(8, 4, 32, TILE)
        store(step).start()


    @pl.when((step >= NORMS_AT) & (step < COLUMNS_AT))
    def _():
        block = step - NORMS_AT
        rows = pl.ds(pl.multiple_of(block * OUT_TILE, OUT_TILE), OUT_TILE)
        advance((cot, middle, branch), block, COLUMNS_AT - NORMS_AT)
        grad_middle, low = norms_back(
            total_ref[rows],
            cot.block(block),
            middle.block(block),
            branch.block(block),
            vec_ref,
            sums_ref,
        )
        grad_middle_ref[rows] = grad_middle
        low_ref[rows] = low

    @pl.when((step >= COLUMNS_AT) & (step < HEADS_AT))
    def _():
        block = step - COLUMNS_AT
        columns = pl.ds(pl.multiple_of(block * TILE, TILE), TILE)
        advance((attended,), block, HEADS_AT - COLUMNS_AT)

        @pl.when(block == 0)
        def _():
            fetches[2].wait()
            fetches[3].wait()

        grad_out, delta = heads_back(
            low_ref[...],
            out_weight_ref[columns],
            hs_ref[0:1, columns],
            attended.block(block)[...],
        )
        ga_ref[:, columns] = grad_out
        delta_sum_ref[block, 0:1] = column_sum(delta)
        turned = delta.T
        for head in range(4):
            delta_ref[4 * block + head] = turned[head : head + 1]
        out_grad_ref[:, columns] = dot_nn(scaled_turned_ref[...], low_ref[:, columns]).astype(BF)

    @pl.when(step == HEADS_AT - 1)
    def _():
        total_ref[...] = jnp.zeros_like(total_ref)


    @pl.when((step >= HEADS_AT) & (step < TOKENS_AT))
    def _():
        pair = step - HEADS_AT
        columns = pl.ds(pl.multiple_of(pair * 128, 128), 128)
        advance((proj, lse, in_weight), pair, pairs)

        @pl.when(pair == 0)
        def _():
            fetches[4].wait()

        for part, starts in enumerate(((0, 3 * TILE), (TILE, 2 * TILE))):
            if part == 1:
                reduce_step(tick + 1)
            attention_back_keys(
                starts,
                cross_flag(lengths_ref, total_ref),
                *[proj.block(pair).at[:, pl.ds(index * 128, 128)] for index in range(3)],
                ga_ref.at[:, columns],
                lse.block(pair),
                [delta_ref[2 * pair], delta_ref[2 * pair + 1]],
                dq_ref,
                dk_ref,
                dv_ref,
            )
        query_sum, value_sum = in_back_pair(
            dq_ref,
            dk_ref,
            dv_ref,
            in_weight.block(pair)[...],
            turned_ref,
            out_grad_ref.at[:, columns],
            chunk_ref.at[pair % 2].reshape(8, 4, 32, 512),
            total_ref,
        )
        sums_ref[0:1, columns] = query_sum
        sums_ref[1:2, columns] = value_sum
        stage(0, "own", take_own, tick + 1)

    @pl.when((step >= TOKENS_AT) & (step < TOKENS_AT + 4))
    def _():
        block = step - TOKENS_AT
        rows = pl.ds(pl.multiple_of(block * TILE, TILE), TILE)
        advance((tokens,), block, 4)

        @pl.when(block >= 2)
        def _():
            put_tokens(block - 2).wait()

        result, gain_grad, shift_grad = tokens_back(
            tokens.block(block)[...], total_ref[rows], grad_middle_ref[rows], vec_ref[3:4]
        )
        tokens_grad_ref[block % 2] = result
        put_tokens(block).start()
        sums_ref[3:4] += gain_grad
        sums_ref[4:5] += shift_grad


    @pl.when(step == VECTORS_AT)
    def _():
        for y in range(2):
            for z in range(4):
                own = slice((2 * z + y) * 128, (2 * z + y + 1) * 128)
                for index in range(9):
                    lanes = slice(index % 4 * 128, index % 4 * 128 + 128)
                    row = 6 + index // 4
                    units_ref[8, row : row + 1, lanes] = sums_ref[index : index + 1, own]
                for x in range(2):
                    for c in range(2):
                        unit = 4 * y + 2 * x + c
                        units_ref[8, 0:3] = units_ref[unit, 0:3]
                        if (y, z, x, c) == (0, 0, 0, 0):
                            units_ref[8, 3:4] = sums_ref[9:10, 0:UNITS]
                            units_ref[8, 4:5] = sums_ref[9:10, UNITS : 2 * UNITS]
                            for block in range(4):
                                lanes = slice(block * 128, block * 128 + 128)
                                units_ref[8, 5:6, lanes] = delta_sum_ref[block, 0:1]
                        small.source[y, x, c, z] = units_ref[8].astype(BF)
        small.stage0()

    for index, action in enumerate((small.stage1, small.stage2, small.stage3)):

        @pl.when(step == VECTORS_AT + 1 + index)
        def _():
            action()

    @pl.when(step == VECTORS_AT + 4)
    def _():
        vec_out[...] = small.stage4()
        for block in range(2, 4):
            put_tokens(block).wait()


def back_part(
    lengths,
    act,
    slope,
    e,
    stats,
    up_near,
    up_late,
    feed_turned,
    unit_grad,
    down_grad,
    cotangent,
    middle,
    branch,
    scaled_turned,
    attended,
    out_weights,
    vectors,
    head_lanes,
    projected,
    lse,
    weights,
    turned,
    tokens,
):
    rows, width = tokens.shape
    pairs = width // 128

    return pl.pallas_call(
        back_kernel,
        grid=(BACK_STEPS,),
        in_specs=[
            pl.BlockSpec(memory_space=pltpu.SMEM),
            whole(unit_grad.shape),
            whole(vectors.shape),
            whole(head_lanes.shape),
            *[ANY] * 19,
        ],
        out_specs=[
            whole((4, 4, 32, 1024)),
            whole((8, 4, 32, 512)),
            whole((32, 3 * width)),
            whole((32, width)),
            whole((16, 512)),
            ANY,
            ANY,
        ],
        out_shape=[
            jax.ShapeDtypeStruct((4, 4, 32, 1024), BF),
            jax.ShapeDtypeStruct((8, 4, 32, 512), BF),
            jax.ShapeDtypeStruct((32, 3 * width), F32),
            jax.ShapeDtypeStruct((32, width), F32),
            jax.ShapeDtypeStruct((16, 512), F32),
            jax.ShapeDtypeStruct((rows, width), BF),
            jax.ShapeDtypeStruct((2, 2, 2, 8, 4, 32, UNITS), BF),
        ],
        scratch_shapes=[
            pltpu.VMEM((3, 2, rows, UNITS), BF),
            pltpu.VMEM((2, width, UNITS), BF),
            pltpu.VMEM((rows, 128), F32),
            pltpu.VMEM((width, rows), BF),
            pltpu.VMEM((2, OUT_TILE, width), BF),
            pltpu.VMEM((2, 2, OUT_TILE, width), F32),
            pltpu.VMEM((width, rows), BF),
            pltpu.VMEM((2, rows, TILE), F32),
            pltpu.VMEM((width, width), BF),
            pltpu.VMEM((2, rows, 384), BF),
            pltpu.VMEM((2, 8, rows), F32),
            pltpu.VMEM((2, width, 384), BF),
            pltpu.VMEM((width, rows), BF),
            pltpu.VMEM((2, TILE, width), BF),
            pltpu.VMEM((2, TILE, width), BF),
            pltpu.VMEM((8, 4, 32, UNITS), BF),
            pltpu.VMEM((rows, width), F32),
            pltpu.VMEM((rows, width), BF),
            pltpu.VMEM((width, width), BF),
            pltpu.VMEM((rows, width), BF),
            pltpu.VMEM((rows, width), F32),
            pltpu.VMEM((2 * pairs, 1, rows), F32),
            pltpu.VMEM((4, 8, 128), F32),
            pltpu.VMEM((16, width), F32),
            pltpu.VMEM((9, 16, UNITS), F32),
            pltpu.VMEM((rows, 128), F32),
            pltpu.VMEM((rows, 128), F32),
            pltpu.VMEM((rows, 128), F32),
            pltpu.VMEM((2, 2, 2, 2, 4, 32, 512), BF),
            pltpu.SemaphoreType.DMA((13, 2)),
            pltpu.SemaphoreType.DMA((6,)),
            *Reduction.scratch(),
            *SmallReduction.scratch(),
        ],
        compiler_params=params(collective_id=1, has_side_effects=True),
        name="back_part",
    )(
        lengths,
        unit_grad,
        vectors,
        head_lanes,
        act,
        slope,
        e,
        stats,
        up_near,
        up_late,
        feed_turned,
        down_grad.reshape(2, 2, 2, 4, 4, 32, width),
        cotangent,
        middle,
        branch,
        scaled_turned,
        attended,
        out_weights,
        projected,
        lse,
        weights,
        turned,
        tokens,
    )


def layer(staged, tokens, cotangent, lengths, attn, up, down, unit_vec, head_scale, down_bias):
    rows, width = tokens.shape
    heads = head_scale.shape[0]
    pairs = width // 128
    if staged:
        in_weight, out_weight, vec_block = attn
        (
            turned,
            projected,
            scaled,
            scaled_turned,
            attended,
            lse,
            vectors,
            head_lanes,
            weights,
            out_weights,
            up,
            unit_vec,
        ) = first_part(
            lengths, tokens, in_weight, vec_block, out_weight, up, unit_vec, head_scale[None, :]
        )
        weights = weights.reshape(width, 3 * width)
        out_weights = out_weights.reshape(width, width)
        unit_vec = unit_vec.reshape(-1, unit_vec.shape[-2], UNITS)
        branch, middle, feed_turned, act, slope, stats, up_late, down_near = second_part(
            scaled, out_weights, vectors, tokens, up, unit_vec, down
        )
        mixed, down_grad, e, stats, unit_grad, _ = third_part(
            act, stats, unit_vec, down_near, cotangent, middle, down_bias[None, :]
        )
    else:
        weights, out_weights, vectors = attn
        scale = head_scale.astype(F32)
        head_lanes = jnp.repeat(scale, width // heads)[None, :]
        first, projected, scaled, attended, lse = plain_first(
            lengths, tokens, weights, vectors, head_lanes
        )
        branch, middle, feed = out_proj(scaled, out_weights, vectors, tokens)
        act, slope, stats = up_pass(feed, up, unit_vec)
        mixed, down_grad, e, stats, unit_grad = down_pass(
            act, stats, unit_vec, down, cotangent, middle, down_bias[None, :]
        )
    if staged:
        down_total, up_total, in_total, out_total, vec_shares, tokens_grad, _ = back_part(
            lengths,
            act,
            slope,
            e,
            stats,
            up,
            up_late,
            feed_turned,
            unit_grad,
            down_grad,
            cotangent,
            middle,
            branch,
            scaled_turned,
            attended,
            out_weights,
            vectors,
            head_lanes,
            projected,
            lse,
            weights,
            turned,
            tokens,
        )
        return mixed, tokens_grad, down_total, up_total, in_total, out_total, vec_shares
    up_grad, up_bias_grad, grad_feed = up_back(
        act, slope, e, stats, up, feed
    )
    grad_middle, ga, out_grad, delta, sums = out_back(
        grad_feed,
        cotangent,
        middle,
        branch,
        scaled,
        attended,
        out_weights,
        vectors,
        head_lanes,
    )
    chunks, proj_bias, tokens_grad, pre_sums = in_back(
        lengths,
        projected,
        ga,
        lse,
        delta.reshape(pairs, 2, rows),
        weights,
        first,
        out_grad,
        tokens,
        vectors[3:4],
        grad_middle,
    )
    scale_grad = jnp.sum(delta, axis=1) / scale
    vec_grads = [
        proj_bias[:, 0].reshape(width),
        proj_bias[:, 1].reshape(width),
        sums[2],
        pre_sums[0],
        pre_sums[1],
        sums[5],
        sums[6],
        sums[7],
        sums[8],
    ]
    unit_grads = [up_bias_grad[:, 0], unit_grad[:, 0], unit_grad[:, 1]]
    return mixed, tokens_grad, chunks, up_grad, down_grad, vec_grads, unit_grads, sums[9], scale_grad


def body(
    axes,
    tokens,
    cotangent,
    lengths,
    in_weight,
    query_bias,
    value_bias,
    out_weight,
    out_bias,
    head_scale,
    pre_gain,
    pre_bias,
    post_gain,
    post_bias,
    feed_gain,
    feed_bias,
    up_weight,
    up_bias,
    mid_gain,
    mid_bias,
    down_weight,
    down_bias,
):
    planes, wide = axes
    every = ("dp", "wide")
    staged = (planes, wide) == (4, 8)
    rows, width = tokens.shape
    units = down_weight.shape[0] * wide
    steps = units // UNITS
    share = in_weight.shape[0]
    columns = [
        query_bias,
        value_bias,
        out_bias,
        pre_gain,
        pre_bias,
        post_gain,
        post_bias,
        feed_gain,
        feed_bias,
    ]
    index = lax.broadcasted_iota(jnp.int32, (32, up_bias.shape[0]), 0)
    unit_rows = jnp.where(index == 0, up_bias[None, :], jnp.zeros((), BF))
    unit_rows = jnp.where(index == 1, mid_gain[None, :], unit_rows)
    unit_rows = jnp.where(index == 2, mid_bias[None, :], unit_rows)
    if staged:
        index = lax.broadcasted_iota(jnp.int32, (32, share), 0)
        vec_block = jnp.zeros((32, share), BF)
        for row, column in enumerate(columns):
            vec_block = jnp.where(index == row, column[None, :], vec_block)
        attn = (in_weight, out_weight, vec_block)
        up, unit_vec, down = up_weight, unit_rows, down_weight
    else:
        flat = jnp.concatenate(columns).reshape(len(columns), share)
        attn = (
            lax.all_gather(in_weight, every, axis=0, tiled=True),
            lax.all_gather(out_weight, every, axis=0, tiled=True),
            jnp.pad(
                lax.all_gather(flat, every, axis=1, tiled=True), ((0, 16 - len(columns)), (0, 0))
            ).astype(F32),
        )
        up = lax.all_gather(up_weight, "wide", axis=1, tiled=True)
        up = up.reshape(width, steps, UNITS).transpose(1, 0, 2)
        unit_vec = lax.all_gather(unit_rows, "wide", axis=1, tiled=True)
        unit_vec = unit_vec.reshape(32, steps, UNITS).transpose(1, 0, 2)
        down = lax.all_gather(down_weight, "wide", axis=0, tiled=True)
        down = down.reshape(steps, UNITS, width)
    results = layer(
        staged,
        tokens,
        cotangent,
        lengths,
        attn,
        up,
        down,
        unit_vec,
        head_scale,
        down_bias,
    )
    heads = head_scale.shape[0]
    pairs = width // 128
    if staged:
        mixed, tokens_grad, down_total, up_total, in_total, out_total, vec_shares = results
        up_total = up_total.astype(F32).reshape(width, UNITS)
        down_total = down_total.astype(F32).reshape(UNITS, width)
        unit_totals = [vec_shares[index] for index in range(3)]
        down_sum = vec_shares[3:5].reshape(width)
        scale_sum = vec_shares[5].reshape(4, 128)[:, :4].reshape(heads) / head_scale.astype(F32)
        offset = share * lax.rem(lax.axis_index("wide"), 128 // share)
        own = vec_shares[6:9].reshape(12, 128)
        own = lax.dynamic_slice(own, (0, offset), (len(columns), share))
        vec_totals = [own[index] for index in range(len(columns))]
    else:
        (mixed, tokens_grad, chunks, up_grad, down_grad, vec_grads, unit_grads) = results[:7]
        down_sum, scale_sum = results[7:]

        def scatter(value, axis=0, over=every):
            return lax.psum_scatter(value, over, scatter_dimension=axis, tiled=True)

        def both_ways(value, axis):
            part = scatter(value.astype(BF), axis, "wide")
            return lax.psum(part, "dp").astype(F32)

        up_total = both_ways(up_grad.transpose(1, 0, 2).reshape(width, units), 1)
        down_total = both_ways(down_grad.reshape(units, width), 0)
        unit_totals = [
            lax.psum(scatter(item.reshape(units), 0, "wide"), "dp") for item in unit_grads
        ]
        down_sum, scale_sum = lax.psum((down_sum, scale_sum), every)
        vec_totals = [scatter(item) for item in vec_grads]
        natural = chunks.transpose(0, 2, 1, 3, 4).reshape(pairs, width, 512)
        in_total = natural[:, :, :384].reshape(pairs, width, 3, 128)
        in_total = scatter(in_total.transpose(1, 2, 0, 3).reshape(width, 3 * width).astype(F32))
        out_total = scatter(
            natural[:, :, 384:].transpose(1, 0, 2).reshape(width, width).astype(F32)
        )
    return (
        mixed,
        tokens_grad,
        in_total,
        vec_totals[0],
        vec_totals[1],
        out_total,
        vec_totals[2],
        scale_sum,
        vec_totals[3],
        vec_totals[4],
        vec_totals[5],
        vec_totals[6],
        vec_totals[7],
        vec_totals[8],
        up_total,
        unit_totals[0],
        unit_totals[1],
        unit_totals[2],
        down_total,
        down_sum,
    )


def solution(mesh):
    by_all = P(("dp", "wide"))
    rows_all = P(("dp", "wide"), None)
    axes = (mesh.shape["dp"], mesh.shape["wide"])
    return jax.shard_map(
        functools.partial(body, axes),
        mesh=mesh,
        in_specs=(
            rows_all,
            rows_all,
            rows_all,
            rows_all,
            by_all,
            by_all,
            rows_all,
            by_all,
            P(),
            by_all,
            by_all,
            by_all,
            by_all,
            by_all,
            by_all,
            P(None, "wide"),
            P("wide"),
            P("wide"),
            P("wide"),
            P("wide", None),
            P(),
        ),
        out_specs=(
            rows_all,
            rows_all,
            rows_all,
            by_all,
            by_all,
            rows_all,
            by_all,
            P(),
            by_all,
            by_all,
            by_all,
            by_all,
            by_all,
            by_all,
            P(None, "wide"),
            P("wide"),
            P("wide"),
            P("wide"),
            P("wide", None),
            P(),
        ),
        check_vma=False,
    )
```

profile of v0, /device:TPU:0, one launch (start us, length us, event | category | flops | bytes accessed | tf_op | source)
XLA Modules:
  0.0 341.1 jit_solution(16406671327515909908)
XLA Ops:
  0.7 1.5 select_select_fusion.1.vec_ref
  2.2 1.4 select_select_fusion.unit_ref
  3.6 83.1 %first_part.1 = (bf16[1024,1024]{1,0:T(8,128)(2,1)}, bf16[8,1024,384]{2,1,0:T(8,128)(2,1)}, bf16[1024,1024]{1,0:T(8,128)(2,1)}, bf16[1024,1024]{1,0:T(8,128)(2,1...) custom-call(s32[1,2]{1,0:T(1,128)} %lengths_ref.3, ...), custom_call_target="tpu_custom_call" | custom-call | tf_op jit(solution)/shard_map/first_part/pallas_call | solution.py:1554
  86.7 0.0 copy-start.6
  86.7 42.9 %second_part.1 = (f32[1024,1024]{1,0:T(8,128)}, f32[1024,1024]{1,0:T(8,128)}, bf16[1024,1024]{1,0:T(8,128)(2,1)}, bf16[8,1024,512]{2,1,0:T(8,128)(2,1)}, bf16[8,...) custom-call(bf16[1024,1024]{1,0:T(8,128)(2,1)} %get-tuple-element.51, ...), custom_call_target="tpu_custom_call" | custom-call | tf_op jit(solution)/shard_map/second_part/pallas_call | solution.py:1700
  129.6 0.0 copy-done.6
  129.6 0.6 broadcast_in_dim.109.shift_ref
  130.2 42.8 %third_part.1 = (bf16[1024,1024]{1,0:T(8,128)(2,1)}, bf16[8,512,1024]{2,1,0:T(8,128)(2,1)}, bf16[8,1024,512]{2,1,0:T(8,128)(2,1)}, f32[1024,128]{1,0:T(8,128)}, ...) custom-call(bf16[8,1024,512]{2,1,0:T(8,128)(2,1)} %get-tuple-element.56.act_ref.act_all, ...), custom_call_target="tpu_custom_call" | custom-call | tf_op jit(solution)/shard_map/third_part/pallas_call | solution.py:1812
  173.0 155.9 %back_part.1 = (bf16[4,4,32,1024]{3,2,1,0:T(8,128)(2,1)}, bf16[8,4,32,512]{3,2,1,0:T(8,128)(2,1)}, f32[32,3072]{1,0:T(8,128)}, f32[32,1024]{1,0:T(8,128)}, f32[1...) custom-call(s32[1,2]{1,0:T(1,128)} %lengths_ref.3, ...), custom_call_target="tpu_custom_call" | custom-call | tf_op jit(solution)/shard_map/back_part/pallas_call | solution.py:2271
  328.9 0.0 copy-start.2
  328.9 2.9 bitcast_convert_fusion
  331.8 0.0 copy-done.2
  331.8 1.7 bitcast_convert_fusion.1
  333.5 0.0 copy-done.5
  333.5 0.6 dynamic-slice_bitcast_fusion
  334.2 0.6 fusion
  334.8 0.1 reshape.90
  334.9 0.5 convert_divide_fusion
  335.4 0.6 copy.41
  336.0 1.3 copy.46
  337.3 1.0 copy-done.1
  338.3 1.3 copy.47
  339.7 0.7 copy.48
  340.4 0.7 copy.49
  (18 shorter events, 0.1 us)
Async XLA Ops:
  86.7 42.9 %copy-start.6 = (bf16[1024]{0:T(1024)(128)(2,1)S(1)}, bf16[1024]{0:T(1024)(128)(2,1)}, u32[]{:S(2)}) copy-start(bf16[1024]{0:T(1024)(128)(2,1)} %param.41) | copy-start | bytes 6148
  328.9 2.9 copy-start.2
  331.8 1.7 copy-start.5
  331.8 3.0 copy-start.7
  331.8 4.2 %copy-start = (bf16[1024,1024]{1,0:T(8,128)(2,1)S(1)}, bf16[1024,1024]{1,0:T(8,128)(2,1)}, u32[]{:S(2)}) copy-start(bf16[1024,1024]{1,0:T(8,128)(2,1)} %get-tuple-element.123) | copy-start | bytes 6291460
  336.0 2.3 copy-start.1
  338.3 1.3 copy-start.3
  338.3 2.1 copy-start.4
where the time goes:
time: 342 us; the launch traced here: 341 us
  Pallas kernels  325 us (95%)
  other arithmetic  8.01 us (2%)
  local copies, waits for them, and re-layouts  7.62 us (2%)
    pallas_call x1, Pallas kernels, back_part(): pl.pallas_call(back_kernel, grid=(BACK_STEPS,), in_specs=[pl.BlockSpec(me...  156 us
    pallas_call x1, Pallas kernels, first_part(): pl.pallas_call(first_kernel, grid=(pairs + 1,), in_specs=[pl.BlockSpec(me...  83.1 us
    pallas_call x1, Pallas kernels, second_part(): pl.pallas_call(functools.partial(second_kernel, steps * UNITS), grid=(lea...  42.9 us
    pallas_call x1, Pallas kernels, third_part(): pl.pallas_call(functools.partial(third_kernel, steps * UNITS), grid=(step...  42.8 us

commit v1 on v0

--- a/solution.py
+++ b/solution.py
@@ -73,13 +73,6 @@
     return jnp.where(lengths_ref[0, 0] == rows_ref.shape[0], 0.0, MASKED)
 
 
-def stacked(value, low_lanes):
-    zero = jnp.zeros_like(value)
-    return jnp.concatenate(
-        [jnp.where(low_lanes, value, zero), jnp.where(low_lanes, zero, value)], axis=0
-    )
-
-
 def attention_pair(cross, q_ref, k_ref, v_ref, scale, scaled_ref, out_ref, lse_ref, vext_ref):
     rows = q_ref.shape[0]
     half = rows // 2
@@ -92,10 +85,11 @@
     vext_ref[:, 128:] = jnp.ones((rows, 128), BF)
     for start in range(0, rows, TILE):
         stop = start + TILE
-        both = dot_nt(stacked(q_ref[start:stop], low_lanes), k_ref[:stop])
-        peaks, weights = [], []
+        query = q_ref[start:stop]
+        results = []
         for head in range(2):
-            raw = both[head * TILE : (head + 1) * TILE]
+            mine = low_lanes if head == 0 else ~low_lanes
+            raw = dot_nt(jnp.where(mine, query, jnp.zeros_like(query)), k_ref[:stop])
             parts = []
             if start >= half:
                 parts.append((raw[:, :half], cross))
@@ -110,19 +104,18 @@
                 if shift is not None:
                     top = top + shift
                 peak = top if peak is None else jnp.maximum(peak, top)
-            peaks.append(peak)
-            pieces = []
+            weights = []
             for piece, shift in parts:
                 level = peak if shift is None else peak - shift
-                pieces.append(jnp.exp2((piece - level) * factor).astype(BF))
-            weights.append(pieces[0] if len(pieces) == 1 else jnp.concatenate(pieces, axis=1))
-        both = dot_nn(jnp.concatenate(weights, axis=0), vext_ref[:stop])
-        total = jnp.where(low_lanes, both[:TILE, 128:], both[TILE:, 128:])
-        peak = jnp.where(low_lanes, peaks[0], peaks[1])
-        mixed = jnp.where(low_lanes, both[:TILE, :128], both[TILE:, :128]) / total
+                weights.append(jnp.exp2((piece - level) * factor).astype(BF))
+            weights = weights[0] if len(weights) == 1 else jnp.concatenate(weights, axis=1)
+            both = dot_nn(weights, vext_ref[:stop])
+            total = both[:, 128:]
+            results.append((both[:, :128] / total, peak * factor + jnp.log2(total)))
+        mixed = jnp.where(low_lanes, results[0][0], results[1][0])
         out_ref[start:stop] = mixed
         scaled_ref[start:stop] = (mixed * scale).astype(BF)
-        lse = (peak * factor + jnp.log2(total)).T
+        lse = jnp.where(low_lanes, results[0][1], results[1][1]).T
         lse_ref[0, 0:1, start:stop] = lse[0:1]
         lse_ref[0, 1:2, start:stop] = lse[64:65]
 
@@ -652,57 +645,49 @@
     )
 
 
-def attention_back_keys(
-    starts, cross, q_ref, k_ref, v_ref, ga_ref, lse_ref, deltas, dq_ref, dk_ref, dv_ref
+def attention_back_head(
+    head, cross, q_ref, k_ref, v_ref, ga_ref, lse_ref, delta, dq_ref, dk_ref, dv_ref
 ):
     rows = q_ref.shape[0]
     half = rows // 2
     factor = LOG2E * 64 ** (-0.5)
     low_lanes = lax.broadcasted_iota(jnp.int32, (1, 128), 1) < 64
+    mine = low_lanes if head == 0 else ~low_lanes
     above = lax.broadcasted_iota(jnp.int32, (TILE, TILE), 0) <= lax.broadcasted_iota(
         jnp.int32, (TILE, TILE), 1
     )
-
-    def pick(both):
-        return jnp.where(low_lanes, both[:TILE], both[TILE:])
-
-    for start in starts:
+    zero = jnp.zeros((rows, 128), BF)
+    query = jnp.where(mine, q_ref[...], zero)
+    grad = jnp.where(mine, ga_ref[...], zero)
+    key_own = jnp.where(mine, k_ref[...], zero)
+    for start in range(0, rows, TILE):
         stop = start + TILE
-        keys = k_ref[start:stop]
-        keys_apart = stacked(keys, low_lanes)
-        values_apart = stacked(v_ref[start:stop], low_lanes)
-        dk = jnp.zeros((TILE, 128), F32)
-        dv = jnp.zeros((TILE, 128), F32)
-        for left, right in ((start, half), (half, rows)) if start < half else ((start, rows),):
-            raw = dot_nt(keys_apart, q_ref[left:right])
-            grad_weights = dot_nt(values_apart, ga_ref[left:right])
-            weights, grad_scores = [], []
-            for head in range(2):
-                mine = slice(head * TILE, (head + 1) * TILE)
-                level = lse_ref[head : head + 1, left:right]
-                if start < half <= left:
-                    level = level - cross
-                exponent = raw[mine] * factor - level
-                if left == start:
-                    first = jnp.where(above, exponent[:, :TILE], MASKED)
-                    exponent = (
-                        first
-                        if right - left == TILE
-                        else jnp.concatenate([first, exponent[:, TILE:]], axis=1)
-                    )
-                weight = jnp.exp2(exponent)
-                weights.append(weight.astype(BF))
-                delta = deltas[head][:, left:right]
-                grad_scores.append((weight * (grad_weights[mine] - delta)).astype(BF))
-            dv = dv + pick(dot_nn(jnp.concatenate(weights, axis=0), ga_ref[left:right]))
-            dk = dk + pick(dot_nn(jnp.concatenate(grad_scores, axis=0), q_ref[left:right]))
-            dq = jnp.where(low_lanes, dot_tn(grad_scores[0], keys), dot_tn(grad_scores[1], keys))
-            if start == 0:
-                dq_ref[left:right] = dq
-            else:
-                dq_ref[left:right] += dq
-        dk_ref[start:stop] = dk
-        dv_ref[start:stop] = dv
+        raw = dot_nt(k_ref[start:stop], query[start:])
+        level = lse_ref[head : head + 1, start:]
+        parts = [jnp.where(above, raw[:, :TILE] * factor - level[:, :TILE], MASKED)]
+        if start < half:
+            if stop < half:
+                parts.append(raw[:, TILE : half - start] * factor - level[:, TILE : half - start])
+            parts.append(raw[:, half - start :] * factor - (level[:, half - start :] - cross))
+        elif stop < rows:
+            parts.append(raw[:, TILE:] * factor - level[:, TILE:])
+        exponent = parts[0] if len(parts) == 1 else jnp.concatenate(parts, axis=1)
+        weights = jnp.exp2(exponent)
+        grad_weights = dot_nt(v_ref[start:stop], grad[start:])
+        grad_scores = (weights * (grad_weights - delta[:, start:])).astype(BF)
+        dv = dot_nn(weights.astype(BF), grad[start:])
+        dk = dot_nn(grad_scores, query[start:])
+        dq = dot_tn(grad_scores, key_own[start:stop])
+        if head == 0:
+            dv_ref[start:stop] = dv
+            dk_ref[start:stop] = dk
+        else:
+            dv_ref[start:stop] += dv
+            dk_ref[start:stop] += dk
+        if head == 0 and start == 0:
+            dq_ref[...] = dq
+        else:
+            dq_ref[start:] += dq
 
 
 def in_back_pair(dq_ref, dk_ref, dv_ref, weights, turned_ref, out_grad_ref, chunk_ref, total_ref):
@@ -761,20 +746,20 @@
         turned_ref[...] = first_ref[...].T
         total_ref[...] = jnp.zeros_like(total_ref)
 
-    deltas = [delta_ref[0, head : head + 1] for head in range(2)]
-    attention_back_keys(
-        range(0, rows_all, TILE),
-        cross_flag(lengths_ref, tokens_ref),
-        q_ref,
-        k_ref,
-        v_ref,
-        ga_ref,
-        lse_ref.at[0],
-        deltas,
-        dq_ref,
-        dk_ref,
-        dv_ref,
-    )
+    for head in range(2):
+        attention_back_head(
+            head,
+            cross_flag(lengths_ref, tokens_ref),
+            q_ref,
+            k_ref,
+            v_ref,
+            ga_ref,
+            lse_ref.at[0],
+            delta_ref[0, head : head + 1],
+            dq_ref,
+            dk_ref,
+            dv_ref,
+        )
     weights = jnp.concatenate([wq_ref[...], wk_ref[...], wv_ref[...]], axis=1)
     query_sum, value_sum = in_back_pair(
         dq_ref, dk_ref, dv_ref, weights, turned_ref, out_grad_ref, chunk_ref.at[0], total_ref
@@ -2158,16 +2143,16 @@
         def _():
             fetches[4].wait()
 
-        for part, starts in enumerate(((0, 3 * TILE), (TILE, 2 * TILE))):
-            if part == 1:
+        for head in range(2):
+            if head == 1:
                 reduce_step(tick + 1)
-            attention_back_keys(
-                starts,
+            attention_back_head(
+                head,
                 cross_flag(lengths_ref, total_ref),
                 *[proj.block(pair).at[:, pl.ds(index * 128, 128)] for index in range(3)],
                 ga_ref.at[:, columns],
                 lse.block(pair),
-                [delta_ref[2 * pair], delta_ref[2 * pair + 1]],
+                delta_ref[2 * pair + head],
                 dq_ref,
                 dk_ref,
                 dv_ref,

time: 342 us -> 341 us (level)
  no operation moved by 1% of the time
where the time goes in v1:
time: 341 us; the launch traced here: 340 us
  Pallas kernels  324 us (95%)
  other arithmetic  8.01 us (2%)
  local copies, waits for them, and re-layouts  7.62 us (2%)
    pallas_call x1, Pallas kernels, back_part(): pl.pallas_call(back_kernel, grid=(BACK_STEPS,), in_specs=[pl.BlockSpec(me...  156 us
    pallas_call x1, Pallas kernels, first_part(): pl.pallas_call(first_kernel, grid=(pairs + 1,), in_specs=[pl.BlockSpec(me...  82.2 us
    pallas_call x1, Pallas kernels, third_part(): pl.pallas_call(functools.partial(third_kernel, steps * UNITS), grid=(step...  42.9 us
    pallas_call x1, Pallas kernels, second_part(): pl.pallas_call(functools.partial(second_kernel, steps * UNITS), grid=(lea...  42.6 us

profile of v1, /device:TPU:0, one launch (start us, length us, event | category | flops | bytes accessed | tf_op | source)
XLA Modules:
  0.0 340.3 jit_solution(6289254406858112622)
XLA Ops:
  0.7 1.5 select_select_fusion.1.vec_ref
  2.2 1.4 select_select_fusion.unit_ref
  3.6 82.2 %first_part.1 = (bf16[1024,1024]{1,0:T(8,128)(2,1)}, bf16[8,1024,384]{2,1,0:T(8,128)(2,1)}, bf16[1024,1024]{1,0:T(8,128)(2,1)}, bf16[1024,1024]{1,0:T(8,128)(2,1...) custom-call(s32[1,2]{1,0:T(1,128)} %lengths_ref.3, ...), custom_call_target="tpu_custom_call" | custom-call | tf_op jit(solution)/shard_map/first_part/pallas_call | solution.py:1539
  85.9 0.0 copy-start.6
  85.9 42.6 %second_part.1 = (f32[1024,1024]{1,0:T(8,128)}, f32[1024,1024]{1,0:T(8,128)}, bf16[1024,1024]{1,0:T(8,128)(2,1)}, bf16[8,1024,512]{2,1,0:T(8,128)(2,1)}, bf16[8,...) custom-call(bf16[1024,1024]{1,0:T(8,128)(2,1)} %get-tuple-element.51, ...), custom_call_target="tpu_custom_call" | custom-call | tf_op jit(solution)/shard_map/second_part/pallas_call | solution.py:1685
  128.5 0.0 copy-done.6
  128.5 0.6 broadcast_in_dim.109.shift_ref
  129.1 42.9 %third_part.1 = (bf16[1024,1024]{1,0:T(8,128)(2,1)}, bf16[8,512,1024]{2,1,0:T(8,128)(2,1)}, bf16[8,1024,512]{2,1,0:T(8,128)(2,1)}, f32[1024,128]{1,0:T(8,128)}, ...) custom-call(bf16[8,1024,512]{2,1,0:T(8,128)(2,1)} %get-tuple-element.56.act_ref.act_all, ...), custom_call_target="tpu_custom_call" | custom-call | tf_op jit(solution)/shard_map/third_part/pallas_call | solution.py:1797
  172.0 156.1 %back_part.1 = (bf16[4,4,32,1024]{3,2,1,0:T(8,128)(2,1)}, bf16[8,4,32,512]{3,2,1,0:T(8,128)(2,1)}, f32[32,3072]{1,0:T(8,128)}, f32[32,1024]{1,0:T(8,128)}, f32[1...) custom-call(s32[1,2]{1,0:T(1,128)} %lengths_ref.3, ...), custom_call_target="tpu_custom_call" | custom-call | tf_op jit(solution)/shard_map/back_part/pallas_call | solution.py:2256
  328.2 0.0 copy-start.2
  328.2 2.9 bitcast_convert_fusion
  331.1 0.0 copy-done.2
  331.1 1.7 bitcast_convert_fusion.1
  332.8 0.0 copy-done.5
  332.8 0.6 dynamic-slice_bitcast_fusion
  333.4 0.6 fusion
  334.0 0.1 reshape.90
  334.1 0.5 convert_divide_fusion
  334.6 0.6 copy.41
  335.2 1.3 copy.46
  336.6 1.0 copy-done.1
  337.6 1.3 copy.47
  338.9 0.7 copy.48
  339.7 0.7 copy.49
  (18 shorter events, 0.1 us)
Async XLA Ops:
  85.9 42.7 %copy-start.6 = (bf16[1024]{0:T(1024)(128)(2,1)S(1)}, bf16[1024]{0:T(1024)(128)(2,1)}, u32[]{:S(2)}) copy-start(bf16[1024]{0:T(1024)(128)(2,1)} %param.41) | copy-start | bytes 6148
  328.2 2.9 copy-start.2
  331.1 1.7 copy-start.5
  331.1 3.0 copy-start.7
  331.1 4.2 %copy-start = (bf16[1024,1024]{1,0:T(8,128)(2,1)S(1)}, bf16[1024,1024]{1,0:T(8,128)(2,1)}, u32[]{:S(2)}) copy-start(bf16[1024,1024]{1,0:T(8,128)(2,1)} %get-tuple-element.123) | copy-start | bytes 6291460
  335.2 2.3 copy-start.1
  337.6 1.3 copy-start.3
  337.6 2.1 copy-start.4

commit v2 on v1

--- a/solution.py
+++ b/solution.py
@@ -1422,6 +1422,7 @@
                 copy.start()
             if group == 0:
                 early[0].start()
+        out.wide.start()
         scale = hs_ref[...].astype(F32)
         for pair in range(width // 128):
             own = slice(pair * 128, (pair + 1) * 128)
@@ -1440,12 +1441,15 @@
         early[0].relay(1)
         early[0].relay(2)
         early[1].relay(0)
+        out.wide.relay(0)
         early[1].relay(1)
+        out.wide.relay(1)
         for copy in across[1]:
             copy.wait_recv()
         late.start()
         early[1].relay(2)
-        out.wide.start()
+        out.wide.relay(2)
+        out.start_across()
         unit.start()
         for part in early:
             part.finish()
@@ -1471,16 +1475,11 @@
             @pl.when(step == 2 + stage)
             def _():
                 late.relay(stage)
-                out.wide.relay(stage)
                 unit.relay(stage)
 
     @pl.when(step == 2)
     def _():
         up.start()
-
-    @pl.when(step == 4)
-    def _():
-        out.start_across()
 
     @pl.when(step == 5)
     def _():

time: 341 us -> 333 us (0.977)
  Pallas kernels: 324 us -> 315 us
    pallas_call x1, Pallas kernels: 82.2 us -> 73.7 us  [first_part(): pl.pallas_call(first_kernel, grid=(pairs + 1,), in_specs=[pl.BlockSpec(me...]
where the time goes in v2:
time: 333 us; the launch traced here: 332 us
  Pallas kernels  315 us (95%)
  other arithmetic  8.01 us (2%)
  local copies, waits for them, and re-layouts  7.62 us (2%)
    pallas_call x1, Pallas kernels, back_part(): pl.pallas_call(back_kernel, grid=(BACK_STEPS,), in_specs=[pl.BlockSpec(me...  156 us
    pallas_call x1, Pallas kernels, first_part(): pl.pallas_call(first_kernel, grid=(pairs + 1,), in_specs=[pl.BlockSpec(me...  73.7 us
    pallas_call x1, Pallas kernels, second_part(): pl.pallas_call(functools.partial(second_kernel, steps * UNITS), grid=(lea...  43.3 us
    pallas_call x1, Pallas kernels, third_part(): pl.pallas_call(functools.partial(third_kernel, steps * UNITS), grid=(step...  42.2 us

profile of v2, /device:TPU:0, one launch (start us, length us, event | category | flops | bytes accessed | tf_op | source)
XLA Modules:
  0.0 331.9 jit_solution(5580392989322366780)
XLA Ops:
  0.7 1.5 select_select_fusion.1.vec_ref
  2.2 1.4 select_select_fusion.unit_ref
  3.6 73.7 %first_part.1 = (bf16[1024,1024]{1,0:T(8,128)(2,1)}, bf16[8,1024,384]{2,1,0:T(8,128)(2,1)}, bf16[1024,1024]{1,0:T(8,128)(2,1)}, bf16[1024,1024]{1,0:T(8,128)(2,1...) custom-call(s32[1,2]{1,0:T(1,128)} %lengths_ref.3, ...), custom_call_target="tpu_custom_call" | custom-call | tf_op jit(solution)/shard_map/first_part/pallas_call | solution.py:1538
  77.4 0.0 copy-start.6
  77.4 43.3 %second_part.1 = (f32[1024,1024]{1,0:T(8,128)}, f32[1024,1024]{1,0:T(8,128)}, bf16[1024,1024]{1,0:T(8,128)(2,1)}, bf16[8,1024,512]{2,1,0:T(8,128)(2,1)}, bf16[8,...) custom-call(bf16[1024,1024]{1,0:T(8,128)(2,1)} %get-tuple-element.51, ...), custom_call_target="tpu_custom_call" | custom-call | tf_op jit(solution)/shard_map/second_part/pallas_call | solution.py:1684
  120.7 0.0 copy-done.6
  120.7 0.6 broadcast_in_dim.109.shift_ref
  121.3 42.2 %third_part.1 = (bf16[1024,1024]{1,0:T(8,128)(2,1)}, bf16[8,512,1024]{2,1,0:T(8,128)(2,1)}, bf16[8,1024,512]{2,1,0:T(8,128)(2,1)}, f32[1024,128]{1,0:T(8,128)}, ...) custom-call(bf16[8,1024,512]{2,1,0:T(8,128)(2,1)} %get-tuple-element.56.act_ref.act_all, ...), custom_call_target="tpu_custom_call" | custom-call | tf_op jit(solution)/shard_map/third_part/pallas_call | solution.py:1796
  163.5 156.2 %back_part.1 = (bf16[4,4,32,1024]{3,2,1,0:T(8,128)(2,1)}, bf16[8,4,32,512]{3,2,1,0:T(8,128)(2,1)}, f32[32,3072]{1,0:T(8,128)}, f32[32,1024]{1,0:T(8,128)}, f32[1...) custom-call(s32[1,2]{1,0:T(1,128)} %lengths_ref.3, ...), custom_call_target="tpu_custom_call" | custom-call | tf_op jit(solution)/shard_map/back_part/pallas_call | solution.py:2255
  319.8 2.9 bitcast_convert_fusion
  322.7 1.7 bitcast_convert_fusion.1
  324.3 0.0 copy-done.5
  324.4 0.6 dynamic-slice_bitcast_fusion
  325.0 0.6 fusion
  325.6 0.1 reshape.90
  325.7 0.5 convert_divide_fusion
  326.2 0.6 copy.41
  326.8 0.0 copy-done
  326.8 1.3 copy.46
  328.1 1.0 copy-done.1
  329.2 1.3 copy.47
  330.5 0.0 copy-done.3
  330.5 0.7 copy.48
  331.2 0.7 copy.49
  (18 shorter events, 0.1 us)
Async XLA Ops:
  77.4 43.3 %copy-start.6 = (bf16[1024]{0:T(1024)(128)(2,1)S(1)}, bf16[1024]{0:T(1024)(128)(2,1)}, u32[]{:S(2)}) copy-start(bf16[1024]{0:T(1024)(128)(2,1)} %param.41) | copy-start | bytes 6148
  319.8 2.9 copy-start.2
  322.7 1.7 copy-start.5
  322.7 3.0 copy-start.7
  322.7 4.2 %copy-start = (bf16[1024,1024]{1,0:T(8,128)(2,1)S(1)}, bf16[1024,1024]{1,0:T(8,128)(2,1)}, u32[]{:S(2)}) copy-start(bf16[1024,1024]{1,0:T(8,128)(2,1)} %get-tuple-element.123) | copy-start | bytes 6291460
  326.8 2.3 copy-start.1
  329.2 1.3 copy-start.3
  329.2 2.1 copy-start.4

commit v3 on v2

--- a/solution.py
+++ b/solution.py
@@ -1167,8 +1167,10 @@
 class NearGather:
     copies = 3
 
-    def __init__(self, place, source, target, send, recv, first, last):
+    def __init__(self, place, source, target, send, recv, first, last, rows=None):
         slot = target.at[place.y, place.x, place.c]
+        if rows is not None:
+            source, slot = source.at[rows], slot.at[rows]
         self.all = [
             pltpu.make_async_remote_copy(
                 src_ref=source,
@@ -1380,7 +1382,13 @@
             late = WideGather(place, blocks(pl.ds(0, 4)), 32, send_in, recv_in, first + 3)
     orders = (place.z, *place.ranks)
     out = PlanesLast(place, out_ref, out_all, send_out, recv_out, local.at[2])
-    up = NearGather(place, up_ref, up_all, send_ff, recv_ff, count, local.at[3])
+    ups = [
+        NearGather(place, up_ref, up_all, send_ff, recv_ff, first, local.at[sem], rows)
+        for first, sem, rows in (
+            (count, 3, pl.ds(0, width // 4)),
+            (count + NearGather.copies, 5, pl.ds(width // 4, width - width // 4)),
+        )
+    ]
     unit = WideGather(
         place, blocks_of(unit_all), 32, send_ff, recv_ff, 0, unit_ref, local.at[4]
     )
@@ -1423,6 +1431,7 @@
             if group == 0:
                 early[0].start()
         out.wide.start()
+        ups[0].start()
         scale = hs_ref[...].astype(F32)
         for pair in range(width // 128):
             own = slice(pair * 128, (pair + 1) * 128)
@@ -1479,7 +1488,7 @@
 
     @pl.when(step == 2)
     def _():
-        up.start()
+        ups[1].start()
 
     @pl.when(step == 5)
     def _():
@@ -1523,7 +1532,8 @@
             copy.wait()
         out.finish()
         unit.finish()
-        up.finish()
+        for part in ups:
+            part.finish()
 
 
 def first_part(lengths, tokens, in_weight, vec, out_weight, up_weight, unit_rows, head_scale):
@@ -1583,7 +1593,7 @@
             pltpu.VMEM((rows, 256), BF),
             *dma_sems(6 + 3 * WideGather.copies),
             *dma_sems(PlanesLast.copies),
-            *dma_sems(WideGather.copies + NearGather.copies),
+            *dma_sems(WideGather.copies + 2 * NearGather.copies),
             pltpu.SemaphoreType.DMA((44,)),
         ],
         compiler_params=params(collective_id=0, has_side_effects=True),

time: 333 us -> 329 us (0.988)
  Pallas kernels: 315 us -> 311 us
where the time goes in v3:
time: 329 us; the launch traced here: 328 us
  Pallas kernels  311 us (95%)
  other arithmetic  8.01 us (2%)
  local copies, waits for them, and re-layouts  7.62 us (2%)
    pallas_call x1, Pallas kernels, back_part(): pl.pallas_call(back_kernel, grid=(BACK_STEPS,), in_specs=[pl.BlockSpec(me...  154 us
    pallas_call x1, Pallas kernels, first_part(): pl.pallas_call(first_kernel, grid=(pairs + 1,), in_specs=[pl.BlockSpec(me...  72.3 us
    pallas_call x1, Pallas kernels, second_part(): pl.pallas_call(functools.partial(second_kernel, steps * UNITS), grid=(lea...  43.4 us
    pallas_call x1, Pallas kernels, third_part(): pl.pallas_call(functools.partial(third_kernel, steps * UNITS), grid=(step...  42.2 us

profile of v3, /device:TPU:0, one launch (start us, length us, event | category | flops | bytes accessed | tf_op | source)
XLA Modules:
  0.0 327.9 jit_solution(11482454950577521111)
XLA Ops:
  0.7 1.5 select_select_fusion.1.vec_ref
  2.2 1.4 select_select_fusion.unit_ref
  3.6 72.3 %first_part.1 = (bf16[1024,1024]{1,0:T(8,128)(2,1)}, bf16[8,1024,384]{2,1,0:T(8,128)(2,1)}, bf16[1024,1024]{1,0:T(8,128)(2,1)}, bf16[1024,1024]{1,0:T(8,128)(2,1...) custom-call(s32[1,2]{1,0:T(1,128)} %lengths_ref.3, ...), custom_call_target="tpu_custom_call" | custom-call | tf_op jit(solution)/shard_map/first_part/pallas_call | solution.py:1548
  75.9 0.0 copy-start.6
  75.9 43.4 %second_part.1 = (f32[1024,1024]{1,0:T(8,128)}, f32[1024,1024]{1,0:T(8,128)}, bf16[1024,1024]{1,0:T(8,128)(2,1)}, bf16[8,1024,512]{2,1,0:T(8,128)(2,1)}, bf16[8,...) custom-call(bf16[1024,1024]{1,0:T(8,128)(2,1)} %get-tuple-element.51, ...), custom_call_target="tpu_custom_call" | custom-call | tf_op jit(solution)/shard_map/second_part/pallas_call | solution.py:1694
  119.4 0.0 copy-done.6
  119.4 0.6 broadcast_in_dim.109.shift_ref
  120.0 42.2 %third_part.1 = (bf16[1024,1024]{1,0:T(8,128)(2,1)}, bf16[8,512,1024]{2,1,0:T(8,128)(2,1)}, bf16[8,1024,512]{2,1,0:T(8,128)(2,1)}, f32[1024,128]{1,0:T(8,128)}, ...) custom-call(bf16[8,1024,512]{2,1,0:T(8,128)(2,1)} %get-tuple-element.56.act_ref.act_all, ...), custom_call_target="tpu_custom_call" | custom-call | tf_op jit(solution)/shard_map/third_part/pallas_call | solution.py:1806
  162.1 153.6 %back_part.1 = (bf16[4,4,32,1024]{3,2,1,0:T(8,128)(2,1)}, bf16[8,4,32,512]{3,2,1,0:T(8,128)(2,1)}, f32[32,3072]{1,0:T(8,128)}, f32[32,1024]{1,0:T(8,128)}, f32[1...) custom-call(s32[1,2]{1,0:T(1,128)} %lengths_ref.3, ...), custom_call_target="tpu_custom_call" | custom-call | tf_op jit(solution)/shard_map/back_part/pallas_call | solution.py:2265
  315.7 0.0 copy-start.2
  315.7 2.9 bitcast_convert_fusion
  318.6 0.0 copy-done.2
  318.6 1.7 bitcast_convert_fusion.1
  320.3 0.0 copy-done.5
  320.3 0.6 dynamic-slice_bitcast_fusion
  321.0 0.6 fusion
  321.6 0.1 reshape.90
  321.7 0.5 convert_divide_fusion
  322.2 0.6 copy.41
  322.8 1.3 copy.46
  324.1 1.0 copy-done.1
  325.1 1.3 copy.47
  326.5 0.7 copy.48
  327.2 0.7 copy.49
  (18 shorter events, 0.1 us)
Async XLA Ops:
  75.9 43.5 %copy-start.6 = (bf16[1024]{0:T(1024)(128)(2,1)S(1)}, bf16[1024]{0:T(1024)(128)(2,1)}, u32[]{:S(2)}) copy-start(bf16[1024]{0:T(1024)(128)(2,1)} %param.41) | copy-start | bytes 6148
  315.7 2.9 copy-start.2
  318.6 1.7 copy-start.5
  318.6 3.0 copy-start.7
  318.6 4.2 %copy-start = (bf16[1024,1024]{1,0:T(8,128)(2,1)S(1)}, bf16[1024,1024]{1,0:T(8,128)(2,1)}, u32[]{:S(2)}) copy-start(bf16[1024,1024]{1,0:T(8,128)(2,1)} %get-tuple-element.123) | copy-start | bytes 6291460
  322.8 2.3 copy-start.1
  325.1 1.3 copy-start.3
  325.1 2.1 copy-start.4
